TPU v7x, 256 devices: a whole 4x4x8 slice. The times are simulated.
256 devices in a mesh: space: 32 (over z, x_lo, core), inj: 8 (over y, x_hi).
Axes of the slice: x: 4 (x_hi: 2, x_lo: 2; x = x_hi * 2 + x_lo), y: 4, z: 8, core: 2. Of those that a mesh axis runs over, the one named last changes fastest.
Arguments:
- conductivity: float32 [192, 64, 128], P('space'), may hold values from 0.05 to 2
- start_potential: float32 [16, 192, 64, 128], P('inj', 'space'), may hold values from -6 to 6
- start_adjoint: float32 [16, 192, 64, 128], P('inj', 'space'), may hold values from -6 to 6
- inj_cells: int32 [16, 2], P('inj'), may hold values from 0 to 1572863
- dipole_cells: int32 [8, 1024, 2, 128], P('inj', 'space'), may hold values from 0 to 49151
- owner_tile: int32 [8, 1024, 1], P('inj', 'space'), may hold values from 0 to 31; in each aligned block of 32 rows (0 to 31, 32 to 63, ..., all dimensions but the last counted through in order) at most 2 rows name the same one
- live_count: int32 [8, 1024], P('inj', 'space'), may hold values from 1 to 128, 81920 in all within a row
- observed: float32 [8, 1024, 2, 128], P('inj', 'space'), may hold values from -6 to 6
Outputs:
- gradient: float32 [192, 64, 128], P('space', 'inj')
- residual: float32 [8, 1024, 2, 128], P('inj', 'space')
Inputs may be any that keep to these rules, and one draw needn't show every extreme that they name: `owner_tile`: of the rows of one device, no more than 2 name the same tile, and on some device some tile is named by exactly 2 rows. The first live_count slots of a block are in use, the rest are padding.
All inputs are finite; a program needn't handle non-finite values.
Results may differ from a plain program's by a relative error of at most 0.0003.
Values sent between devices are 32-bit elements; how exact they have to be, the bound alone decides.
A program may use at most 128 MiB of HBM per device.

v0:
```python
import math

import jax
import jax.numpy as jnp
from jax import lax
from jax.sharding import PartitionSpec as P

current_amp = 4.0
sweep_weights = [
    1.0 / (1.0 + 0.9 * math.cos((2 * step_k + 1) * math.pi / 6.0)) for step_k in range(3)
]


def extended(shard, sides, width):
    for axis, dim in sides:
        devices, length = (lax.axis_size(axis), shard.shape[dim])
        up = [(i, (i + 1) % devices) for i in range(devices - 1)]
        down = [(j, i) for i, j in up]
        last = lax.slice_in_dim(shard, length - width, length, axis=dim)
        initial = lax.slice_in_dim(shard, 0, width, axis=dim)
        before = lax.ppermute(last, axis, up)
        after = lax.ppermute(initial, axis, down)
        shard = jnp.concatenate([before, shard, after], axis=dim)
    return shard


def forward_cell(values, which_axis):
    length = values.shape[which_axis]
    interior = lax.slice_in_dim(values, 1, length, axis=which_axis)
    border = jnp.zeros_like(lax.slice_in_dim(values, 0, 1, axis=which_axis))
    return jnp.concatenate([interior, border], axis=which_axis)


def backward_cell(values, which_axis):
    length = values.shape[which_axis]
    interior = lax.slice_in_dim(values, 0, length - 1, axis=which_axis)
    border = jnp.zeros_like(lax.slice_in_dim(values, 0, 1, axis=which_axis))
    return jnp.concatenate([border, interior], axis=which_axis)


def conductances(sigma):
    face_xp = 0.5 * (sigma + forward_cell(sigma, 0))
    face_xm = 0.5 * (sigma + backward_cell(sigma, 0))
    face_yp = 0.5 * (sigma + forward_cell(sigma, 1))
    face_ym = 0.5 * (sigma + backward_cell(sigma, 1))
    face_zp = 0.5 * (sigma + forward_cell(sigma, 2))
    face_zm = 0.5 * (sigma + backward_cell(sigma, 2))
    diagonal = face_xp + face_xm + face_yp + face_ym + face_zp + face_zm
    return (face_xp, face_xm, face_yp, face_ym, face_zp, face_zm, diagonal)


def operate(values, faces, leading):
    beside_all = faces[0] * forward_cell(values, leading) + faces[1] * backward_cell(
        values, leading
    )
    beside_all = (
        beside_all
        + faces[2] * forward_cell(values, leading + 1)
        + faces[3] * backward_cell(values, leading + 1)
    )
    beside_all = (
        beside_all
        + faces[4] * forward_cell(values, leading + 2)
        + faces[5] * backward_cell(values, leading + 2)
    )
    return faces[6] * values - beside_all


def relax_each(potential, source_center, faces):
    diag_center = faces[6][1:-1]
    for weight in sweep_weights:
        widened = extended(potential, (("space", 1),), 1)
        applied = operate(widened, faces, 1)[:, 1:-1]
        potential = potential + weight * ((source_center - applied) / diag_center)
    return potential


def local_term(rim_potential, rim_adjoint):
    potential = rim_potential[:, 1:-1]
    adjoint = rim_adjoint[:, 1:-1]
    total = (potential - rim_potential[:, 2:]) * (adjoint - rim_adjoint[:, 2:])
    total = total + (potential - rim_potential[:, :-2]) * (adjoint - rim_adjoint[:, :-2])
    for leading in (2, 3):
        for mover in (forward_cell, backward_cell):
            total = total + (potential - mover(potential, leading)) * (
                adjoint - mover(adjoint, leading)
            )
    return jnp.sum(-0.5 * total, axis=0)


def body(
    conductivity,
    start_potential,
    start_adjoint,
    inj_cells,
    dipole_cells,
    owner_tile,
    live_count,
    observed,
):
    rows_x, rows_y, rows_z = conductivity.shape
    groups_here = start_potential.shape[0]
    tile_count = lax.axis_size("space")
    tile_index = lax.axis_index("space")
    margin = 1
    sigma_wide = extended(conductivity, (("space", 0),), margin + 1)
    faces = tuple((member[1:-1] for member in conductances(sigma_wide)))
    extent = rows_x + 2 * margin
    global_row = tile_index * rows_x - margin + jnp.arange(extent, dtype=jnp.int32)
    plane_ids = lax.broadcasted_iota(
        jnp.int32, (rows_y, rows_z), 0
    ) * rows_z + lax.broadcasted_iota(jnp.int32, (rows_y, rows_z), 1)
    cell_ids = (global_row[:, None, None] * (rows_y * rows_z) + plane_ids[None])[None]
    hits_plus = (cell_ids == inj_cells[:, 0, None, None, None]).astype(jnp.float32)
    hits_minus = (cell_ids == inj_cells[:, 1, None, None, None]).astype(jnp.float32)
    source_wide = current_amp * (hits_plus - hits_minus)
    potential = relax_each(start_potential, source_wide[:, 1:-1], faces)
    blocks = owner_tile.shape[1]
    capacity = max(2, blocks // tile_count + 1)
    slots = tile_count * capacity
    owners = owner_tile[0, :, 0]
    block_ids = jnp.arange(blocks, dtype=jnp.int32)
    earlier = (owners[None, :] == owners[:, None]) & (block_ids[None, :] < block_ids[:, None])
    slot_of = owners * capacity + jnp.sum(earlier.astype(jnp.int32), axis=1)
    matches = slot_of[None, :] == jnp.arange(slots, dtype=jnp.int32)[:, None]
    filled = jnp.any(matches, axis=1)
    source_block = jnp.sum(jnp.where(matches, block_ids[None, :], 0), axis=1)
    send_pairs = jnp.where(filled[:, None, None], dipole_cells[0][source_block], 0).reshape(
        tile_count, capacity, 2, -1
    )
    send_live = jnp.where(filled, live_count[0][source_block], 0).reshape(tile_count, capacity)
    send_measured = jnp.where(filled[:, None, None], observed[0][source_block], 0.0).reshape(
        tile_count, capacity, groups_here, -1
    )
    potential_flat = potential.reshape(groups_here, -1)
    pairs_in = lax.all_to_all(send_pairs, "space", split_axis=0, concat_axis=0, tiled=True)
    live_in = lax.all_to_all(send_live, "space", split_axis=0, concat_axis=0, tiled=True)
    measured_in = lax.all_to_all(send_measured, "space", split_axis=0, concat_axis=0, tiled=True)
    electrodes = pairs_in.shape[-1]
    plus_side = jnp.moveaxis(potential_flat[:, pairs_in[:, :, 0, :]], 0, 2)
    minus_side = jnp.moveaxis(potential_flat[:, pairs_in[:, :, 1, :]], 0, 2)
    keep_slot = (jnp.arange(electrodes, dtype=jnp.int32)[None, None, :] < live_in[:, :, None])[
        :, :, None, :
    ]
    misfit = jnp.where(keep_slot, plus_side - minus_side - measured_in, 0.0)
    returned = lax.all_to_all(misfit, "space", split_axis=0, concat_axis=0, tiled=True)
    returned, misfit, pairs_in = (returned, misfit, pairs_in)
    residual_block = returned.reshape(slots, groups_here, -1)[slot_of][None]
    plus_ids = pairs_in[:, :, 0, :].reshape(-1)
    minus_ids = pairs_in[:, :, 1, :].reshape(-1)
    kept_misfit = jnp.moveaxis(misfit, 2, 0).reshape(groups_here, -1)
    adjoint_source = (
        jnp.zeros_like(potential_flat)
        .at[:, plus_ids]
        .add(kept_misfit)
        .at[:, minus_ids]
        .add(-kept_misfit)
    )
    adjoint_source = adjoint_source.reshape(potential.shape)
    adjoint = relax_each(start_adjoint, adjoint_source, faces)
    both_rims = extended(jnp.concatenate([potential, adjoint], axis=0), (("space", 1),), 1)
    rim_potential = both_rims[:groups_here]
    rim_adjoint = both_rims[groups_here:]
    partial_term = local_term(rim_potential, rim_adjoint)
    gradient = lax.psum_scatter(partial_term, "inj", scatter_dimension=1, tiled=True)
    return (gradient, residual_block)


def solution(mesh):
    return jax.shard_map(
        body,
        mesh=mesh,
        in_specs=(
            P("space", None, None),
            P("inj", "space", None, None),
            P("inj", "space", None, None),
            P("inj", None),
            P("inj", "space", None, None),
            P("inj", "space", None),
            P("inj", "space"),
            P("inj", "space", None, None),
        ),
        out_specs=(P("space", "inj", None), P("inj", "space", None, None)),
        check_vma=False,
    )
```

profile of v0, /device:TPU:1, one launch (start us, length us, event | category | flops | bytes accessed | tf_op | source)
XLA Modules:
  0.0 456.0 jit_solution(3467652245106755442)
XLA Ops:
  8.1 4.5 collective-permute-start
  15.5 3.6 collective-permute-start.2
  21.9 3.6 collective-permute-start.8
  29.5 12.9 %all-to-all-start.1 = ((s32[32,1,2]{2,1,0:T(1,128)}), s32[32,1,2]{2,1,0:T(1,128)S(1)}, u32[]{:S(2)}, u32[]{:S(2)}) async-start(s32[32,1,2]{2,1,0:T(1,128)} %bitcast.8), calls=%async_computation.1 | async-start | bytes 32768 | tf_op jit(solution)/shard_map/all_to_all | solution.py:137
  47.4 2.8 all-to-all-done.1
  50.2 5.5 %all-to-all-start = ((s32[32,2,2,128]{3,1,2,0:T(2,128)}), s32[32,2,2,128]{3,1,2,0:T(2,128)}, u32[]{:S(2)}, u32[]{:S(2)}) async-start(s32[32,2,2,128]{3,1,2,0:T(2,128)} %copy.82), calls=%async_computation | async-start | bytes 131072 | tf_op jit(solution)/shard_map/all_to_all | solution.py:136
  55.9 2.2 collective-permute-start.9
  67.7 2.4 collective-permute-start.5
  70.1 10.0 %all-to-all-start.2 = ((f32[32,2,2,128]{3,1,2,0:T(2,128)}), f32[32,2,2,128]{3,1,2,0:T(2,128)}, u32[]{:S(2)}, u32[]{:S(2)}) async-start(f32[32,2,2,128]{3,1,2,0:T(2,128)} %copy.94), calls=%async_computation.2 | async-start | bytes 131072 | tf_op jit(solution)/shard_map/all_to_all | solution.py:138
  84.7 3.5 collective-permute-start.6
  88.3 2.1 collective-permute-start.7
  90.4 3.4 collective-permute-done.7
  94.9 12.7 %copy.88 = f32[2,6,64,128]{0,3,2,1:T(8,128)} copy(f32[2,6,64,128]{3,2,1,0:T(8,128)S(1)} %fusion.55) | data formatting | bytes 786432 | tf_op jit(solution)/shard_map/add | solution.py:74
  107.5 36.0 %gather_fusion.3 = f32[8192,2]{1,0:T(8,128)} fusion(f32[2,49152]{0,1:T(8,128)} %bitcast.55, s32[8192]{0:T(1024)S(1)} %get-tuple-element.86), kind=kCustom, calls=%fused_computation.3 | custom fusion | bytes 163840 | tf_op jit(solution)/shard_map/gather | solution.py:141
  143.6 36.0 %gather_fusion.2 = f32[8192,2]{1,0:T(8,128)} fusion(f32[2,49152]{0,1:T(8,128)} %bitcast.56, s32[8192]{0:T(1024)S(1)} %get-tuple-element.87), kind=kCustom, calls=%fused_computation.2 | custom fusion | bytes 163840 | tf_op jit(solution)/shard_map/gather | solution.py:140
  179.6 5.9 %sub.117 = f32[8192,2]{1,0:T(8,128)} subtract(f32[8192,2]{1,0:T(8,128)} %gather_fusion.2, f32[8192,2]{1,0:T(8,128)} %gather_fusion.3) | non-fusion elementwise | flops 16384 | bytes 196608 | tf_op jit(solution)/shard_map/sub | solution.py:145
  185.4 2.8 copy.92
  189.3 2.6 copy.96
  192.0 2.7 copy.98
  194.7 61.3 %scatter_custom_fusion = f32[2,49152]{0,1:T(8,128)} fusion(s32[8192]{0:T(1024)} %bitcast.70, f32[8192,2]{1,0:T(8,128)} %copy.96, f32[]{:T(128)} %constant.25.clone.1), kind=kCustom, calls=%fused_computation.8 | custom fusion | flops 16384 | bytes 393728 | tf_op jit(solution)/shard_map/scatter-add | solution.py:155
  256.0 66.1 %scatter_fusion = f32[2,49152]{0,1:T(8,128)} fusion(f32[2,49152]{0,1:T(8,128)} %scatter_custom_fusion, s32[8192]{0:T(1024)S(1)} %bitcast.65, f32[8192,2]{1,0:T(8,128)} %copy.98), kind=kCustom, calls=%fused_computation.7 | custom fusion | flops 16384 | bytes 229376 | tf_op jit(solution)/shard_map/scatter-add | solution.py:157
  322.0 14.7 %copy.99 = f32[2,6,64,128]{3,2,1,0:T(8,128)S(1)} copy(f32[2,6,64,128]{0,3,2,1:T(8,128)} %bitcast.54) | data formatting | bytes 786432 | tf_op jit(solution)/shard_map/reshape | solution.py:159
  336.7 2.1 fusion.46
  340.8 2.6 collective-permute-start.11
  343.5 2.9 collective-permute-done.11
  349.4 2.3 collective-permute-start.13
  351.9 5.2 %collective-permute-done.13 = f32[2,1,64,128]{3,2,1,0:T(8,128)S(1)} collective-permute-done((f32[2,1,64,128]{3,2,1,0:T(8,128)S(1)}, f32[2,1,64,128]{3,2,1,0:T(8,128)S(1)}, u32[]{:S(2)}, u32[]{:S(2)}) %collective-permute-start.13) | collective-permute-done | bytes 65568 | tf_op jit(solution)/shard_map/ppermute | solution.py:22
  360.1 3.6 collective-permute-start.15
  364.5 2.6 collective-permute-done.15
  368.9 15.7 %all-to-all-start.3 = ((f32[32,2,2,128]{3,1,2,0:T(2,128)}), f32[32,2,2,128]{3,1,2,0:T(2,128)S(1)}, u32[]{:S(2)}, u32[]{:S(2)}) async-start(f32[32,2,2,128]{3,1,2,0:T(2,128)} %copy.102), calls=%async_computation.4 | async-start | bytes 131072 | tf_op jit(solution)/shard_map/all_to_all | solution.py:146
  384.7 8.3 %all-to-all-done.3 = f32[32,2,2,128]{3,1,2,0:T(2,128)S(1)} async-done(((f32[32,2,2,128]{3,1,2,0:T(2,128)}), f32[32,2,2,128]{3,1,2,0:T(2,128)S(1)}, u32[]{:S(2)}, u32[]{:S(2)}) %all-to-all-start.3) | async-done | bytes 65568 | tf_op jit(solution)/shard_map/all_to_all | solution.py:146
  394.3 54.8 %reduce-scatter.2.cloned.1.call-done = f32[6,8,128]{2,1,0:T(8,128)} async-done(((f32[6,64,128]{2,1,0:T(8,128)}), f32[6,8,128]{2,1,0:T(8,128)}) %reduce-scatter.2.cloned.1.call-update) | async-done | bytes 24592 | tf_op jit(solution)/shard_map/reduce_scatter | solution.py:165
  (150 shorter events, 43.3 us)
Async XLA Ops:
  7.2 35.5 %copy-start = (s32[1,32,2,128]{3,2,1,0:T(2,128)S(1)}, s32[1,32,2,128]{3,2,1,0:T(2,128)}, u32[]{:S(2)}) copy-start(s32[1,32,2,128]{3,2,1,0:T(2,128)} %param.12) | copy-start | bytes 98308
  7.2 52.2 %copy-start.2 = (f32[2,6,64,128]{3,2,1,0:T(8,128)S(1)}, f32[2,6,64,128]{3,2,1,0:T(8,128)}, u32[]{:S(2)}) copy-start(f32[2,6,64,128]{3,2,1,0:T(8,128)} %param.9) | copy-start | bytes 1179652
  8.1 47.7 %collective-permute-start = (f32[2,64,128]{2,1,0:T(8,128)S(1)}, f32[2,64,128]{2,1,0:T(8,128)S(1)}, u32[]{:S(2)}, u32[]{:S(2)}) collective-permute-start(f32[2,64,128]{2,1,0:T(8,128)S(1)} %get-tuple-element.83), channel_id=1, source_target_pairs={{0,8},{8,16},{16,24},{24,32},{32,40},{40,48},{48,56},{56,64},{64,7... | collective-permute-start | bytes 196616 | tf_op jit(solution)/shard_map/ppermute | solution.py:21
  12.6 46.4 %collective-permute-start.1 = (f32[2,64,128]{2,1,0:T(8,128)S(1)}, f32[2,64,128]{2,1,0:T(8,128)S(1)}, u32[]{:S(2)}, u32[]{:S(2)}) collective-permute-start(f32[2,64,128]{2,1,0:T(8,128)S(1)} %get-tuple-element.82), channel_id=1, source_target_pairs={{8,0},{16,8},{24,16},{32,24},{40,32},{48,40},{56,48},{64,56},{72,6... | collective-permute-start | bytes 196616 | tf_op jit(solution)/shard_map/ppermute | solution.py:22
  15.5 43.8 %collective-permute-start.2 = (f32[2,1,64,128]{3,2,1,0:T(8,128)S(1)}, f32[2,1,64,128]{3,2,1,0:T(8,128)S(1)}, u32[]{:S(2)}, u32[]{:S(2)}) collective-permute-start(f32[2,1,64,128]{3,2,1,0:T(8,128)S(1)} %get-tuple-element.75), channel_id=1, source_target_pairs={{0,8},{8,16},{16,24},{24,32},{32,40},{40,48},{48,56},{56,64},{64,7... | collective-permute-start | bytes 196616 | tf_op jit(solution)/shard_map/ppermute | solution.py:21
  19.1 40.3 %collective-permute-start.3 = (f32[2,1,64,128]{3,2,1,0:T(8,128)S(1)}, f32[2,1,64,128]{3,2,1,0:T(8,128)S(1)}, u32[]{:S(2)}, u32[]{:S(2)}) collective-permute-start(f32[2,1,64,128]{3,2,1,0:T(8,128)S(1)} %get-tuple-element.74), channel_id=1, source_target_pairs={{8,0},{16,8},{24,16},{32,24},{40,32},{48,40},{56,48},{64,56},{72,6... | collective-permute-start | bytes 196616 | tf_op jit(solution)/shard_map/ppermute | solution.py:22
  21.9 38.1 %collective-permute-start.8 = (f32[2,1,64,128]{3,2,1,0:T(8,128)S(1)}, f32[2,1,64,128]{3,2,1,0:T(8,128)S(1)}, u32[]{:S(2)}, u32[]{:S(2)}) collective-permute-start(f32[2,1,64,128]{3,2,1,0:T(8,128)S(1)} %get-tuple-element.67), channel_id=1, source_target_pairs={{0,8},{8,16},{16,24},{24,32},{32,40},{40,48},{48,56},{56,64},{64,7... | collective-permute-start | bytes 196616 | tf_op jit(solution)/shard_map/ppermute | solution.py:21
  26.5 3.0 copy-start.14
  29.5 20.7 %all-to-all-start.1 = ((s32[32,1,2]{2,1,0:T(1,128)}), s32[32,1,2]{2,1,0:T(1,128)S(1)}, u32[]{:S(2)}, u32[]{:S(2)}) async-start(s32[32,1,2]{2,1,0:T(1,128)} %bitcast.8), calls=%async_computation.1 | async-start | bytes 32768 | tf_op jit(solution)/shard_map/all_to_all | solution.py:137
  46.1 19.2 %copy-start.9 = (s32[2]{0:T(128)}, s32[2]{0:T(128)S(1)}, u32[]{:S(2)}) copy-start(s32[2]{0:T(128)S(1)} %get-tuple-element.2) | copy-start | bytes 28
  46.1 19.2 %copy-start.11 = (s32[2]{0:T(128)}, s32[2]{0:T(128)S(1)}, u32[]{:S(2)}) copy-start(s32[2]{0:T(128)S(1)} %get-tuple-element.3) | copy-start | bytes 28
  50.2 19.9 %all-to-all-start = ((s32[32,2,2,128]{3,1,2,0:T(2,128)}), s32[32,2,2,128]{3,1,2,0:T(2,128)}, u32[]{:S(2)}, u32[]{:S(2)}) async-start(s32[32,2,2,128]{3,1,2,0:T(2,128)} %copy.82), calls=%async_computation | async-start | bytes 131072 | tf_op jit(solution)/shard_map/all_to_all | solution.py:136
  55.9 6.1 %collective-permute-start.9 = (f32[2,1,64,128]{3,2,1,0:T(8,128)S(1)}, f32[2,1,64,128]{3,2,1,0:T(8,128)S(1)}, u32[]{:S(2)}, u32[]{:S(2)}) collective-permute-start(f32[2,1,64,128]{3,2,1,0:T(8,128)S(1)} %get-tuple-element.66), channel_id=1, source_target_pairs={{8,0},{16,8},{24,16},{32,24},{40,32},{48,40},{56,48},{64,56},{72,6... | collective-permute-start | bytes 196616 | tf_op jit(solution)/shard_map/ppermute | solution.py:22
  62.0 2.5 copy-start.4
  65.8 16.0 %collective-permute-start.4 = (f32[2,1,64,128]{3,2,1,0:T(8,128)S(1)}, f32[2,1,64,128]{3,2,1,0:T(8,128)S(1)}, u32[]{:S(2)}, u32[]{:S(2)}) collective-permute-start(f32[2,1,64,128]{3,2,1,0:T(8,128)S(1)} %get-tuple-element.70), channel_id=1, source_target_pairs={{0,8},{8,16},{16,24},{24,32},{32,40},{40,48},{48,56},{56,64},{64,7... | collective-permute-start | bytes 196616 | tf_op jit(solution)/shard_map/ppermute | solution.py:21
  67.7 14.1 %collective-permute-start.5 = (f32[2,1,64,128]{3,2,1,0:T(8,128)S(1)}, f32[2,1,64,128]{3,2,1,0:T(8,128)S(1)}, u32[]{:S(2)}, u32[]{:S(2)}) collective-permute-start(f32[2,1,64,128]{3,2,1,0:T(8,128)S(1)} %get-tuple-element.71), channel_id=1, source_target_pairs={{8,0},{16,8},{24,16},{32,24},{40,32},{48,40},{56,48},{64,56},{72,6... | collective-permute-start | bytes 196616 | tf_op jit(solution)/shard_map/ppermute | solution.py:22
  70.1 118.2 %all-to-all-start.2 = ((f32[32,2,2,128]{3,1,2,0:T(2,128)}), f32[32,2,2,128]{3,1,2,0:T(2,128)}, u32[]{:S(2)}, u32[]{:S(2)}) async-start(f32[32,2,2,128]{3,1,2,0:T(2,128)} %copy.94), calls=%async_computation.2 | async-start | bytes 131072 | tf_op jit(solution)/shard_map/all_to_all | solution.py:138
  80.1 369.0 %reduce-scatter.2.cloned.1.call-start = ((), (), s32[]{:S(2)}) async-start(), calls=%async_computation.5 | async-start | bytes 221184 | tf_op jit(solution)/shard_map/reduce_scatter | solution.py:165
  81.8 2.4 copy-start.10
  81.8 2.4 copy-start.12
  84.7 5.7 %collective-permute-start.6 = (f32[2,1,64,128]{3,2,1,0:T(8,128)S(1)}, f32[2,1,64,128]{3,2,1,0:T(8,128)S(1)}, u32[]{:S(2)}, u32[]{:S(2)}) collective-permute-start(f32[2,1,64,128]{3,2,1,0:T(8,128)S(1)} %get-tuple-element.68), channel_id=1, source_target_pairs={{0,8},{8,16},{16,24},{24,32},{32,40},{40,48},{48,56},{56,64},{64,7... | collective-permute-start | bytes 196616 | tf_op jit(solution)/shard_map/ppermute | solution.py:21
  88.3 5.6 %collective-permute-start.7 = (f32[2,1,64,128]{3,2,1,0:T(8,128)S(1)}, f32[2,1,64,128]{3,2,1,0:T(8,128)S(1)}, u32[]{:S(2)}, u32[]{:S(2)}) collective-permute-start(f32[2,1,64,128]{3,2,1,0:T(8,128)S(1)} %get-tuple-element.69), channel_id=1, source_target_pairs={{8,0},{16,8},{24,16},{32,24},{40,32},{48,40},{56,48},{64,56},{72,6... | collective-permute-start | bytes 196616 | tf_op jit(solution)/shard_map/ppermute | solution.py:22
  338.8 4.6 %collective-permute-start.10 = (f32[2,1,64,128]{3,2,1,0:T(8,128)S(1)}, f32[2,1,64,128]{3,2,1,0:T(8,128)S(1)}, u32[]{:S(2)}, u32[]{:S(2)}) collective-permute-start(f32[2,1,64,128]{3,2,1,0:T(8,128)S(1)} %get-tuple-element.59), channel_id=1, source_target_pairs={{0,8},{8,16},{16,24},{24,32},{32,40},{40,48},{48,56},{56,64},{64,7... | collective-permute-start | bytes 196616 | tf_op jit(solution)/shard_map/ppermute | solution.py:21
  340.8 5.6 %collective-permute-start.11 = (f32[2,1,64,128]{3,2,1,0:T(8,128)S(1)}, f32[2,1,64,128]{3,2,1,0:T(8,128)S(1)}, u32[]{:S(2)}, u32[]{:S(2)}) collective-permute-start(f32[2,1,64,128]{3,2,1,0:T(8,128)S(1)} %get-tuple-element.60), channel_id=1, source_target_pairs={{8,0},{16,8},{24,16},{32,24},{40,32},{48,40},{56,48},{64,56},{72,6... | collective-permute-start | bytes 196616 | tf_op jit(solution)/shard_map/ppermute | solution.py:22
  347.3 4.5 collective-permute-start.12
  349.4 7.7 %collective-permute-start.13 = (f32[2,1,64,128]{3,2,1,0:T(8,128)S(1)}, f32[2,1,64,128]{3,2,1,0:T(8,128)S(1)}, u32[]{:S(2)}, u32[]{:S(2)}) collective-permute-start(f32[2,1,64,128]{3,2,1,0:T(8,128)S(1)} %get-tuple-element.58), channel_id=1, source_target_pairs={{8,0},{16,8},{24,16},{32,24},{40,32},{48,40},{56,48},{64,56},{72,6... | collective-permute-start | bytes 196616 | tf_op jit(solution)/shard_map/ppermute | solution.py:22
  358.1 26.6 %copy-start.13 = (s32[1,32,1]{1,2,0:T(1,128)S(1)}, s32[1,32,1]{1,2,0:T(1,128)}, u32[]{:S(2)}) copy-start(s32[1,32,1]{1,2,0:T(1,128)} %param.13) | copy-start | bytes 388
  358.1 26.6 %copy-start.15 = (s32[32]{0:T(128)S(1)}, s32[32]{0:T(128)}, u32[]{:S(2)}) copy-start(s32[32]{0:T(128)} %copy-done.14) | copy-start | bytes 388
  358.1 91.0 %copy-start.1 = (s32[1,32,2,128]{3,2,1,0:T(2,128)S(1)}, s32[1,32,2,128]{3,2,1,0:T(2,128)}, u32[]{:S(2)}) copy-start(s32[1,32,2,128]{3,2,1,0:T(2,128)} %param.12) | copy-start | bytes 98308
  358.2 6.3 %collective-permute-start.14 = (f32[4,1,64,128]{3,2,1,0:T(8,128)S(1)}, f32[4,1,64,128]{3,2,1,0:T(8,128)S(1)}, u32[]{:S(2)}, u32[]{:S(2)}) collective-permute-start(f32[4,1,64,128]{3,2,1,0:T(8,128)S(1)} %get-tuple-element.11), channel_id=1, source_target_pairs={{8,0},{16,8},{24,16},{32,24},{40,32},{48,40},{56,48},{64,56},{72,6... | collective-permute-start | bytes 393224 | tf_op jit(solution)/shard_map/ppermute | solution.py:22
  360.1 6.9 %collective-permute-start.15 = (f32[4,1,64,128]{3,2,1,0:T(8,128)S(1)}, f32[4,1,64,128]{3,2,1,0:T(8,128)S(1)}, u32[]{:S(2)}, u32[]{:S(2)}) collective-permute-start(f32[4,1,64,128]{3,2,1,0:T(8,128)S(1)} %get-tuple-element.12), channel_id=1, source_target_pairs={{0,8},{8,16},{16,24},{24,32},{32,40},{40,48},{48,56},{56,64},{64,7... | collective-permute-start | bytes 393224 | tf_op jit(solution)/shard_map/ppermute | solution.py:21
  368.9 24.1 %all-to-all-start.3 = ((f32[32,2,2,128]{3,1,2,0:T(2,128)}), f32[32,2,2,128]{3,1,2,0:T(2,128)S(1)}, u32[]{:S(2)}, u32[]{:S(2)}) async-start(f32[32,2,2,128]{3,1,2,0:T(2,128)} %copy.102), calls=%async_computation.4 | async-start | bytes 131072 | tf_op jit(solution)/shard_map/all_to_all | solution.py:146
  (5 other events, 4.0 us)
Sparse Core Ops, SparseCore 0:
  368.4 80.6 reduce-scatter.1
where the time goes:
time: 458 us; the launch traced here: 456 us
  other arithmetic  146 us (32%)
  local copies, waits for them, and re-layouts  126 us (28%)
  starting transfers between devices  86.4 us (19%)
  waiting for transfers between devices  82.4 us (18%)
  between operations  14.9 us (3%)
    scatter-add x2, other arithmetic, body(): adjoint_source = jnp.zeros_like(potential_flat).at[:, plus_ids].add(kept_...  127 us
    reduce_scatter x1, waiting for transfers between devices, body(): lax.psum_scatter(partial_term, 'inj', scatter_dimension=1, tiled=True)  54.8 us
    gather x1, local copies, waits for them, and re-layouts, body(): minus_side = jnp.moveaxis(potential_flat[:, pairs_in[:, :, 1, :]], 0, 2)  36 us
    gather x1, local copies, waits for them, and re-layouts, body(): plus_side = jnp.moveaxis(potential_flat[:, pairs_in[:, :, 0, :]], 0, 2)  36 us
    ppermute x8, starting transfers between devices, extended(): before = lax.ppermute(last, axis, up)  24.8 us
    ppermute x8, starting transfers between devices, extended(): after = lax.ppermute(initial, axis, down)  17.4 us
    all_to_all x1, starting transfers between devices, body(): lax.all_to_all(misfit, 'space', split_axis=0, concat_axis=0, tiled=True)  15.7 us
    reshape x1, local copies, waits for them, and re-layouts, body(): adjoint_source = adjoint_source.reshape(potential.shape)  14.7 us
  transfers between devices with their start and end apart: 21, of which 9 were waited for; matrix products, arithmetic and copies ran while one was open for 26% of the time, Pallas kernels for 0%

commit v1 on v0

v1 whole, which is shorter than its diff:
```python
import functools
import math

import jax
import jax.numpy as jnp
from jax import lax
from jax.experimental import pallas as pl
from jax.experimental.pallas import tpu as pltpu
from jax.sharding import PartitionSpec as P

MESH = pl.DeviceIdType.MESH
F32 = jnp.float32
BF16 = jnp.bfloat16
HIGHEST = lax.Precision.HIGHEST

current_amp = 4.0
sweep_weights = [
    1.0 / (1.0 + 0.9 * math.cos((2 * step_k + 1) * math.pi / 6.0)) for step_k in range(3)
]

H = 4
PAD = 8


def iota(shape, dim):
    return lax.broadcasted_iota(jnp.int32, shape, dim)


def rows_sum(values):
    return jnp.sum(values, axis=0, keepdims=True)


def kernel(
    n_space, n_inj, nx, ny, nz, blocks,
    sig_in, pot_in, adj_in, inj_cells, owner, live, cells, observed,
    grad_out, res_out,
    sigma, pa, pb, aa, ab, coef, src, asrc, send, recv, ret_send, ret_recv,
    rim, onehot, table, scat, partial, shares,
    local_sem, halo_send, halo_recv, far_send, far_recv, block_send, block_recv,
    ret_send_sem, ret_recv_sem, rim_send, rim_recv, asrc_send, asrc_recv, share_send, share_recv,
):
    me = lax.axis_index("space")
    my_inj = lax.axis_index("inj")
    left = lax.rem(me + n_space - 1, n_space)
    right = lax.rem(me + 1, n_space)
    planes = nx + 2 * H
    rows = pl.ds(PAD, ny)
    half = nx // 2
    tall = half * ny
    wide = 2 * nz
    half_cells = float(half * ny * nz)

    barrier = pltpu.get_barrier_semaphore()

    def greet(d, carry):
        pl.semaphore_signal(barrier, inc=1, device_id=(lax.rem(me + d, n_space), my_inj), device_id_type=MESH)
        return carry

    def greet_inj(d, carry):
        pl.semaphore_signal(barrier, inc=1, device_id=(me, lax.rem(my_inj + d, n_inj)), device_id_type=MESH)
        return carry

    lax.fori_loop(1, n_space, greet, 0)
    lax.fori_loop(1, n_inj, greet_inj, 0)

    locals_ = [
        pltpu.make_async_copy(sig_in, sigma.at[pl.ds(H, nx), rows], local_sem.at[0]),
        pltpu.make_async_copy(pot_in, pa.at[:, pl.ds(H, nx), rows], local_sem.at[1]),
        pltpu.make_async_copy(adj_in, aa.at[:, pl.ds(H, nx), rows], local_sem.at[2]),
    ]
    for copy in locals_:
        copy.start()

    edge = jnp.zeros((PAD, nz), F32)

    def clear(p, carry):
        for low in (0, PAD + ny):
            sigma[p, pl.ds(low, PAD), :] = edge
            for i in range(2):
                for buf in (pa, pb, aa, ab):
                    buf[i, p, pl.ds(low, PAD), :] = edge
        return carry

    lax.fori_loop(0, planes, clear, 0)

    lanes = 4 * blocks
    lane_c = iota((blocks, lanes), 1)
    block_c = lax.rem(lane_c, 2 * blocks) // 2
    field_c = lax.rem(lane_c, 2) + 2 * (lane_c // (2 * blocks))
    row_b = iota((blocks, lanes), 0)
    owners = jnp.broadcast_to(owner[...].astype(F32), (blocks, lanes))
    owner_c = rows_sum(jnp.where(row_b == block_c, owners, 0.0))
    earlier = (owners == owner_c) & (row_b < block_c)
    rank_c = rows_sum(jnp.where(earlier, 1.0, 0.0))
    slot_c = owner_c * 2.0 + rank_c
    target = slot_c * 4.0 + field_c[:1].astype(F32)
    place = jnp.where(iota((n_space * 8, lanes), 0).astype(F32) == target, 1.0, 0.0)

    row_r = iota((lanes, blocks), 0)
    block_r = lax.rem(row_r, 2 * blocks) // 2
    lives = jnp.broadcast_to(live[...].astype(F32), (lanes, blocks))
    live_r = jnp.sum(jnp.where(block_r == iota((lanes, blocks), 1), lives, 0.0), axis=1, keepdims=True)
    data = jnp.concatenate([cells[...].astype(F32) + 1.0, observed[...]], axis=0)
    elec = data.shape[1]
    data = jnp.where(iota((lanes, elec), 1).astype(F32) < live_r, data, 0.0)
    packed = jnp.dot(place, data, precision=HIGHEST, preferred_element_type=F32)
    for t in range(n_space):
        send[t] = packed[8 * t : 8 * t + 8]

    pl.semaphore_wait(barrier, n_space - 1 + n_inj - 1)

    def remote(source, target, send_sem, recv_sem, space, inj):
        return pltpu.make_async_remote_copy(
            src_ref=source, dst_ref=target, send_sem=send_sem, recv_sem=recv_sem,
            device_id=(space, inj), device_id_type=MESH,
        )

    early = [
        remote(sig_in.at[pl.ds(nx - H, H)], sigma.at[pl.ds(0, H), rows], halo_send.at[0], halo_recv.at[0], right, my_inj),
        remote(sig_in.at[pl.ds(0, H)], sigma.at[pl.ds(nx + H, H), rows], halo_send.at[1], halo_recv.at[1], left, my_inj),
        remote(pot_in.at[:, pl.ds(nx - 3, 3)], pa.at[:, pl.ds(H - 3, 3), rows], halo_send.at[2], halo_recv.at[2], right, my_inj),
        remote(pot_in.at[:, pl.ds(0, 3)], pa.at[:, pl.ds(nx + H, 3), rows], halo_send.at[3], halo_recv.at[3], left, my_inj),
    ]
    late = [
        remote(adj_in.at[:, pl.ds(nx - H, H)], aa.at[:, pl.ds(0, H), rows], far_send.at[0], far_recv.at[0], right, my_inj),
        remote(adj_in.at[:, pl.ds(0, H)], aa.at[:, pl.ds(nx + H, H), rows], far_send.at[1], far_recv.at[1], left, my_inj),
    ]
    for copy in early:
        copy.start()

    def send_block(d, carry):
        to = lax.rem(me + d, n_space)
        remote(send.at[to], recv.at[me], block_send, block_recv, to, my_inj).start()
        return carry

    lax.fori_loop(1, n_space, send_block, 0)
    for copy in late:
        copy.start()
    recv[me] = send[me]

    cell_ids = iota((ny, nz), 0) * nz + iota((ny, nz), 1)

    def own_source(p, carry):
        first = (me * nx - H + p) * (ny * nz)
        for i in range(2):
            plus = jnp.where(cell_ids == inj_cells[i, 0] - first, current_amp, 0.0)
            minus = jnp.where(cell_ids == inj_cells[i, 1] - first, current_amp, 0.0)
            src[i, p] = plus - minus
        return carry

    lax.fori_loop(0, planes, own_source, 0)

    def no_halo(buf, lead):
        nothing = jnp.zeros((ny, nz), F32)

        @pl.when(me == 0)
        def _():
            for p in range(H):
                for i in range(lead):
                    if lead == 1:
                        buf[p, rows, :] = nothing
                    else:
                        buf[i, p, rows, :] = nothing

        @pl.when(me == n_space - 1)
        def _():
            for p in range(nx + H, planes):
                for i in range(lead):
                    if lead == 1:
                        buf[p, rows, :] = nothing
                    else:
                        buf[i, p, rows, :] = nothing

    first_lane = iota((ny, nz), 1) == 0
    last_lane = iota((ny, nz), 1) == nz - 1

    locals_[0].wait()
    early[0].wait()
    early[1].wait()
    no_halo(sigma, 1)

    def faces(p, carry):
        here = sigma[p, rows, :]
        zp = jnp.where(last_lane, 0.0, pltpu.roll(here, nz - 1, 1))
        zm = jnp.where(first_lane, 0.0, pltpu.roll(here, 1, 1))
        around = [
            sigma[p + 1, rows, :], sigma[p - 1, rows, :],
            sigma[p, pl.ds(PAD + 1, ny), :], sigma[p, pl.ds(PAD - 1, ny), :], zp, zm,
        ]
        around = [0.5 * (here + value) for value in around]
        diag = around[0] + around[1] + around[2] + around[3] + around[4] + around[5]
        plane = me * nx - H + p
        inside = jnp.where((plane >= 0) & (plane < n_space * nx), 1.0, 0.0)
        inverse = inside / jnp.where(diag > 0.0, diag, 1.0)
        around[4] = jnp.where(last_lane, 0.0, around[4])
        around[5] = jnp.where(first_lane, 0.0, around[5])
        for k in range(6):
            coef[k, p] = around[k] * inverse
        coef[6, p] = inverse
        return carry

    lax.fori_loop(1, planes - 1, faces, 0)

    def sweep(source, old, new, low, high, weight):
        def plane(p, carry):
            c = [coef[k, p] for k in range(7)]
            for i in range(2):
                here = old[i, p, rows, :]
                beside = c[0] * old[i, p + 1, rows, :] + c[1] * old[i, p - 1, rows, :]
                beside = beside + (
                    c[2] * old[i, p, pl.ds(PAD + 1, ny), :] + c[3] * old[i, p, pl.ds(PAD - 1, ny), :]
                )
                beside = beside + (c[4] * pltpu.roll(here, nz - 1, 1) + c[5] * pltpu.roll(here, 1, 1))
                beside = beside + c[6] * source[i, p]
                new[i, p, rows, :] = here + weight * (beside - here)
            return carry

        lax.fori_loop(low, high, plane, 0)

    locals_[1].wait()
    early[2].wait()
    early[3].wait()
    no_halo(pa, 2)
    sweep(src, pa, pb, 2, planes - 2, sweep_weights[0])
    sweep(src, pb, pa, 3, planes - 3, sweep_weights[1])
    sweep(src, pa, pb, H, planes - H, sweep_weights[2])

    rims = [
        remote(pb.at[:, H + nx - 1, rows], rim.at[0], rim_send.at[0], rim_recv.at[0], right, my_inj),
        remote(pb.at[:, H, rows], rim.at[1], rim_send.at[1], rim_recv.at[1], left, my_inj),
    ]
    for copy in rims:
        copy.start()

    for i in range(2):
        for x in range(nx):
            value = pb[i, H + x, rows, :]
            high = value.astype(BF16)
            low = (value - high.astype(F32)).astype(BF16)
            at = (pl.ds(i * tall + (x % half) * ny, ny))
            table[at, pl.ds((x // half) * nz, nz)] = high
            table[at, pl.ds(wide + (x // half) * nz, nz)] = low

    got = pltpu.make_async_copy(recv.at[pl.ds(0, n_space - 1)], recv.at[pl.ds(0, n_space - 1)], block_recv)
    got.wait()

    wide_iota = iota((wide, elec), 0).astype(F32).astype(BF16)
    tall_iota = iota((tall, elec), 0).astype(F32)
    tall_iota16 = tall_iota.astype(BF16)
    one = jnp.ones((wide, elec), BF16)
    none = jnp.zeros((wide, elec), BF16)

    def split_cells(t):
        cell = recv[t] - 1.0
        upper = cell >= half_cells
        within = jnp.where(upper, cell - half_cells, cell)
        tall_at = jnp.floor(within * (1.0 / nz))
        wide_at = within - tall_at * nz + jnp.where(upper, float(nz), 0.0)
        return tall_at, jnp.where(cell < 0.0, -1.0, wide_at)

    def fetch(t, carry):
        tall_at, wide_at = split_cells(t)
        for s in range(2):
            for f in range(2):
                row = jnp.broadcast_to(wide_at[4 * s + f : 4 * s + f + 1], (wide, elec)).astype(BF16)
                onehot[t, :, pl.ds((2 * s + f) * elec, elec)] = jnp.where(wide_iota == row, one, none)
        hot = onehot[t]
        found = jnp.dot(table[:, :wide], hot, preferred_element_type=F32)
        found = found + jnp.dot(table[:, wide:], hot, preferred_element_type=F32)
        out = []
        for s in range(2):
            ends = [[], []]
            for f in range(2):
                row = tall_at[4 * s + f : 4 * s + f + 1]
                here = tall_iota == row
                for i in range(2):
                    piece = found[i * tall : (i + 1) * tall, (2 * s + f) * elec : (2 * s + f + 1) * elec]
                    ends[i].append(rows_sum(jnp.where(here, piece, 0.0)))
            for i in range(2):
                out.append(ends[i][0] - ends[i][1] - recv[t, pl.ds(4 * s + 2 + i, 1), :])
        ret_send[t] = jnp.concatenate(out, axis=0)
        return carry

    lax.fori_loop(0, n_space, fetch, 0)

    def send_ret(d, carry):
        to = lax.rem(me + d, n_space)
        remote(ret_send.at[to], ret_recv.at[me], ret_send_sem, ret_recv_sem, to, my_inj).start()
        return carry

    lax.fori_loop(1, n_space, send_ret, 0)
    ret_recv[me] = ret_send[me]

    scat[...] = jnp.zeros_like(scat)

    def spread(t, carry):
        tall_at, _ = split_cells(t)
        misfit = ret_send[t]
        high = misfit.astype(BF16).astype(F32)
        low = misfit - high
        columns = [[], []]
        for s in range(2):
            for f in range(2):
                sign = 1.0 if f == 0 else -1.0
                row = jnp.broadcast_to(tall_at[4 * s + f : 4 * s + f + 1], (tall, elec)).astype(BF16)
                here = tall_iota16 == row
                for part, value in enumerate((high, low)):
                    pieces = []
                    for i in range(2):
                        amount = jnp.broadcast_to(sign * value[2 * s + i : 2 * s + i + 1], (tall, elec)).astype(BF16)
                        pieces.append(jnp.where(here, amount, jnp.zeros((tall, elec), BF16)))
                    columns[part].append(jnp.concatenate(pieces, axis=0))
        hot = onehot[t]
        total = scat[...]
        for part in range(2):
            total = total + lax.dot_general(
                jnp.concatenate(columns[part], axis=1), hot, (((1,), (1,)), ((), ())),
                preferred_element_type=F32,
            )
        scat[...] = total
        return carry

    lax.fori_loop(0, n_space, spread, 0)
    for i in range(2):
        for x in range(nx):
            asrc[i, H + x] = scat[pl.ds(i * tall + (x % half) * ny, ny), pl.ds((x // half) * nz, nz)]
    around = [
        remote(asrc.at[:, pl.ds(H + nx - 3, 3)], asrc.at[:, pl.ds(1, 3)], asrc_send.at[0], asrc_recv.at[0], right, my_inj),
        remote(asrc.at[:, pl.ds(H, 3)], asrc.at[:, pl.ds(H + nx, 3)], asrc_send.at[1], asrc_recv.at[1], left, my_inj),
    ]
    for copy in around:
        copy.start()

    locals_[2].wait()
    late[0].wait()
    late[1].wait()
    no_halo(aa, 2)
    for copy in rims:
        copy.wait()
    for i in range(2):
        pb[i, H - 1, rows, :] = jnp.where(me == 0, 0.0, rim[0, i])
        pb[i, H + nx, rows, :] = jnp.where(me == n_space - 1, 0.0, rim[1, i])

    for copy in around:
        copy.wait()
    sweep(asrc, aa, ab, 1, planes - 1, sweep_weights[0])
    sweep(asrc, ab, aa, 2, planes - 2, sweep_weights[1])
    sweep(asrc, aa, ab, 3, planes - 3, sweep_weights[2])

    def term(x, carry):
        p = x + H
        total = jnp.zeros((ny, nz), F32)
        for i in range(2):
            here, there = pb[i, p, rows, :], ab[i, p, rows, :]
            pairs = [
                (pb[i, p + 1, rows, :], ab[i, p + 1, rows, :]),
                (pb[i, p - 1, rows, :], ab[i, p - 1, rows, :]),
                (pb[i, p, pl.ds(PAD + 1, ny), :], ab[i, p, pl.ds(PAD + 1, ny), :]),
                (pb[i, p, pl.ds(PAD - 1, ny), :], ab[i, p, pl.ds(PAD - 1, ny), :]),
                tuple(jnp.where(last_lane, 0.0, pltpu.roll(v, nz - 1, 1)) for v in (here, there)),
                tuple(jnp.where(first_lane, 0.0, pltpu.roll(v, 1, 1)) for v in (here, there)),
            ]
            for u, v in pairs:
                total = total + (here - u) * (there - v)
        partial[:, x] = (-0.5 * total).reshape(n_inj, ny // n_inj, nz)
        return carry

    lax.fori_loop(0, nx, term, 0)

    def send_share(d, carry):
        to = lax.rem(my_inj + d, n_inj)
        remote(partial.at[to], shares.at[my_inj], share_send, share_recv, me, to).start()
        return carry

    lax.fori_loop(1, n_inj, send_share, 0)
    shares[my_inj] = partial[my_inj]

    ret_got = pltpu.make_async_copy(ret_recv.at[pl.ds(0, n_space - 1)], ret_recv.at[pl.ds(0, n_space - 1)], ret_recv_sem)
    ret_got.wait()
    lane_j = lax.rem(iota((1, lanes), 1), 2).astype(F32)
    back = jnp.where(iota((n_space * 4, lanes), 0).astype(F32) == slot_c * 2.0 + lane_j, 1.0, 0.0)
    back = jnp.transpose(back)[: 2 * blocks]
    returned = jnp.concatenate([ret_recv[t] for t in range(n_space)], axis=0)
    res_out[...] = jnp.dot(back, returned, precision=HIGHEST, preferred_element_type=F32)

    share_got = pltpu.make_async_copy(shares.at[pl.ds(0, n_inj - 1)], shares.at[pl.ds(0, n_inj - 1)], share_recv)
    share_got.wait()
    total = shares[0]
    for k in range(1, n_inj):
        total = total + shares[k]
    grad_out[...] = total

    pltpu.make_async_copy(send.at[pl.ds(0, n_space - 1)], send.at[pl.ds(0, n_space - 1)], block_send).wait()
    pltpu.make_async_copy(ret_send.at[pl.ds(0, n_space - 1)], ret_send.at[pl.ds(0, n_space - 1)], ret_send_sem).wait()
    pltpu.make_async_copy(partial.at[pl.ds(0, n_inj - 1)], partial.at[pl.ds(0, n_inj - 1)], share_send).wait()


def body(
    conductivity, start_potential, start_adjoint, inj_cells, dipole_cells, owner_tile, live_count, observed,
):
    n_space, n_inj = lax.axis_size("space"), lax.axis_size("inj")
    nx, ny, nz = conductivity.shape
    blocks, elec = observed.shape[1], observed.shape[3]
    planes, tall_rows = nx + 2 * H, ny + 2 * PAD
    wide, tall = 2 * nz, nx // 2 * ny
    anywhere = pl.BlockSpec(memory_space=pl.ANY)
    vmem = pl.BlockSpec(memory_space=pltpu.VMEM)
    smem = pl.BlockSpec(memory_space=pltpu.SMEM)
    field = pltpu.VMEM((2, planes, tall_rows, nz), F32)
    dma = pltpu.SemaphoreType.DMA
    gradient, residual = pl.pallas_call(
        functools.partial(kernel, n_space, n_inj, nx, ny, nz, blocks),
        out_shape=(
            jax.ShapeDtypeStruct((nx, ny // n_inj, nz), F32),
            jax.ShapeDtypeStruct((2 * blocks, elec), F32),
        ),
        in_specs=[anywhere, anywhere, anywhere, smem, vmem, vmem, vmem, vmem],
        out_specs=(vmem, vmem),
        scratch_shapes=[
            pltpu.VMEM((planes, tall_rows, nz), F32),
            field, field, field, field,
            pltpu.VMEM((7, planes, ny, nz), F32),
            pltpu.VMEM((2, planes, ny, nz), F32),
            pltpu.VMEM((2, planes, ny, nz), F32),
            pltpu.VMEM((n_space, 8, elec), F32),
            pltpu.VMEM((n_space, 8, elec), F32),
            pltpu.VMEM((n_space, 4, elec), F32),
            pltpu.VMEM((n_space, 4, elec), F32),
            pltpu.VMEM((2, 2, ny, nz), F32),
            pltpu.VMEM((n_space, wide, 4 * elec), BF16),
            pltpu.VMEM((2 * tall, 2 * wide), BF16),
            pltpu.VMEM((2 * tall, wide), F32),
            pltpu.VMEM((n_inj, nx, ny // n_inj, nz), F32),
            pltpu.VMEM((n_inj, nx, ny // n_inj, nz), F32),
            dma((3,)), dma((4,)), dma((4,)), dma((2,)), dma((2,)), dma, dma,
            dma, dma, dma((2,)), dma((2,)), dma((2,)), dma((2,)), dma, dma,
        ],
        compiler_params=pltpu.CompilerParams(
            collective_id=0, has_side_effects=True, vmem_limit_bytes=48 * 1024 * 1024
        ),
    )(
        conductivity, start_potential, start_adjoint, inj_cells,
        owner_tile.reshape(blocks, 1), live_count,
        dipole_cells.reshape(2 * blocks, elec), observed.reshape(2 * blocks, elec),
    )
    return gradient, residual.reshape(1, blocks, 2, elec)


def solution(mesh):
    return jax.shard_map(
        body,
        mesh=mesh,
        in_specs=(
            P("space", None, None),
            P("inj", "space", None, None),
            P("inj", "space", None, None),
            P("inj", None),
            P("inj", "space", None, None),
            P("inj", "space", None),
            P("inj", "space"),
            P("inj", "space", None, None),
        ),
        out_specs=(P("space", "inj", None), P("inj", "space", None, None)),
        check_vma=False,
    )
```

time: 458 us -> 76.7 us (0.17)
  other arithmetic: 146 us -> 0 us
  local copies, waits for them, and re-layouts: 126 us -> 6.98 us
  starting transfers between devices: 86.4 us -> 0 us
  waiting for transfers between devices: 82.4 us -> 0 us
  Pallas kernels: 0 us -> 68.7 us
  between operations: 14.9 us -> 0.66 us
    scatter-add x2 -> x0, other arithmetic: 127 us -> none  [body(): adjoint_source = jnp.zeros_like(potential_flat).at[:, plus_ids].add(kept_...]
    gather x8 -> x0, local copies, waits for them, and re-layouts: 76.8 us -> none  [the longest x1 36 us: body(): minus_side = jnp.moveaxis(potential_flat[:, pairs_in[:, :, 1, :]], 0, 2)]
    pallas_call x0 -> x1, Pallas kernels: none -> 68.7 us  [body(): pl.pallas_call(functools.partial(kernel, n_space, n_inj, nx, ny, nz, bloc...]
    reduce_scatter x1 -> x0, waiting for transfers between devices: 54.8 us -> none  [body(): lax.psum_scatter(partial_term, 'inj', scatter_dimension=1, tiled=True)]
    all_to_all x4 -> x0, starting transfers between devices: 44.2 us -> none  [the longest x1 15.7 us: body(): lax.all_to_all(misfit, 'space', split_axis=0, concat_axis=0, tiled=True)]
    ppermute x16 -> x0, starting transfers between devices: 42.3 us -> none  [the longest x8 24.8 us: extended(): before = lax.ppermute(last, axis, up)]
    reshape x3 -> x1, local copies, waits for them, and re-layouts: 17.4 us -> 0.09 us  [body(): owner_tile.reshape(blocks, 1)]
    ppermute x16 -> x0, waiting for transfers between devices: 16.4 us -> none  [the longest x8 13.8 us: extended(): after = lax.ppermute(initial, axis, down)]
  transfers between devices with their start and end apart: 21 -> 0, of which waited for: 9 -> 0; matrix products, arithmetic and copies ran while one was open for 26% -> 0% of each run, Pallas kernels for 0% -> 0%
where the time goes in v1:
time: 76.7 us; the launch traced here: 76.4 us
  Pallas kernels  68.7 us (90%)
  local copies, waits for them, and re-layouts  6.98 us (9%)
    pallas_call x1, Pallas kernels, body(): pl.pallas_call(functools.partial(kernel, n_space, n_inj, nx, ny, nz, bloc...  68.7 us
    unnamed x18, local copies, waits for them, and re-layouts  6.9 us

profile of v1, /device:TPU:1, one launch (start us, length us, event | category | flops | bytes accessed | tf_op | source)
XLA Modules:
  0.0 76.4 jit_solution(8541083997441649573)
XLA Ops:
  0.6 0.0 copy-start.7
  0.6 0.6 copy-done.7
  1.3 0.0 copy-start.5
  1.3 0.0 copy-start.6
  1.3 0.1 copy.10.owner
  1.4 0.6 copy-done.5
  2.0 0.0 copy-done.6
  2.0 0.0 copy-start
  2.0 1.0 %copy-done = f32[2,6,64,128]{3,2,1,0:T(8,128)S(1)} copy-done((f32[2,6,64,128]{3,2,1,0:T(8,128)S(1)}, f32[2,6,64,128]{3,2,1,0:T(8,128)}, u32[]{:S(2)}) %copy-start) | copy-done | bytes 393240
  3.0 0.0 copy-start.1
  3.0 1.0 %copy-done.1 = f32[2,6,64,128]{3,2,1,0:T(8,128)S(1)} copy-done((f32[2,6,64,128]{3,2,1,0:T(8,128)S(1)}, f32[2,6,64,128]{3,2,1,0:T(8,128)}, u32[]{:S(2)}) %copy-start.1) | copy-done | bytes 393240
  4.0 0.0 copy-start.2
  4.0 0.9 %copy-done.2 = f32[6,64,128]{2,1,0:T(8,128)S(1)} copy-done((f32[6,64,128]{2,1,0:T(8,128)S(1)}, f32[6,64,128]{2,1,0:T(8,128)}, u32[]{:S(2)}) %copy-start.2) | copy-done | bytes 196632
  4.9 0.0 copy-start.3
  4.9 0.8 copy-done.3
  5.6 0.0 copy-start.4
  5.7 0.8 copy-done.4
  6.4 68.7 %shard_map.95 = (f32[6,8,128]{2,1,0:T(8,128)S(1)}, f32[64,128]{1,0:T(8,128)S(1)}) custom-call(f32[6,64,128]{2,1,0:T(8,128)S(1)} %copy-done.2, f32[2,6,64,128]{3,2,1,0:T(8,128)S(1)} %copy-done, f32[2,6,64,128]{3,2,1,0:T(8,128)S(1)} %copy-done.1, s32[2,2]{1,0:T(2,128)S(1)} %copy-done.5, s32[32,1]{1,0:T(8,128)S(1)} %copy.10.owner, s32[1,32]{1,0:T(1,128)S(1)} %copy-done.6, ...), custom_call_target="tpu_custom_call" | custom-call | tf_op jit(solution)/shard_map/pallas_call | solution.py:411
  75.2 0.6 copy.13
  75.8 0.6 copy.14
Async XLA Ops:
  0.6 0.7 copy-start.7
  1.3 0.7 copy-start.5
  1.3 0.7 copy-start.6
  2.0 1.0 %copy-start = (f32[2,6,64,128]{3,2,1,0:T(8,128)S(1)}, f32[2,6,64,128]{3,2,1,0:T(8,128)}, u32[]{:S(2)}) copy-start(f32[2,6,64,128]{3,2,1,0:T(8,128)} %pot_in.1) | copy-start | bytes 1179652
  3.0 1.0 %copy-start.1 = (f32[2,6,64,128]{3,2,1,0:T(8,128)S(1)}, f32[2,6,64,128]{3,2,1,0:T(8,128)}, u32[]{:S(2)}) copy-start(f32[2,6,64,128]{3,2,1,0:T(8,128)} %adj_in.1) | copy-start | bytes 1179652
  4.0 0.9 %copy-start.2 = (f32[6,64,128]{2,1,0:T(8,128)S(1)}, f32[6,64,128]{2,1,0:T(8,128)}, u32[]{:S(2)}) copy-start(f32[6,64,128]{2,1,0:T(8,128)} %sig_in.1) | copy-start | bytes 589828
  4.9 0.8 copy-start.3
  5.6 0.8 copy-start.4

commit v2 on v1

--- a/solution.py
+++ b/solution.py
@@ -32,9 +32,9 @@
 
 def kernel(
     n_space, n_inj, nx, ny, nz, blocks,
-    sig_in, pot_in, adj_in, inj_cells, owner, live, cells, observed,
+    sig_in, pot_in, adj_in, inj_in, owner_in, live_in, cells_in, observed_in,
     grad_out, res_out,
-    sigma, pa, pb, aa, ab, coef, src, asrc, send, recv, ret_send, ret_recv,
+    inj_cells, owner, live, cells, observed, sigma, pa, pb, aa, ab, coef, src, asrc, send, recv, ret_send, ret_recv,
     rim, onehot, table, scat, partial, shares,
     local_sem, halo_send, halo_recv, far_send, far_recv, block_send, block_recv,
     ret_send_sem, ret_recv_sem, rim_send, rim_recv, asrc_send, asrc_recv, share_send, share_recv,
@@ -49,6 +49,7 @@
     tall = half * ny
     wide = 2 * nz
     half_cells = float(half * ny * nz)
+    group = math.gcd(n_space, 8)
 
     barrier = pltpu.get_barrier_semaphore()
 
@@ -63,12 +64,18 @@
     lax.fori_loop(1, n_space, greet, 0)
     lax.fori_loop(1, n_inj, greet_inj, 0)
 
+    small = [
+        pltpu.make_async_copy(source, target, local_sem.at[3 + k])
+        for k, (source, target) in enumerate(
+            ((inj_in, inj_cells), (owner_in, owner), (live_in, live), (cells_in, cells), (observed_in, observed))
+        )
+    ]
     locals_ = [
         pltpu.make_async_copy(sig_in, sigma.at[pl.ds(H, nx), rows], local_sem.at[0]),
         pltpu.make_async_copy(pot_in, pa.at[:, pl.ds(H, nx), rows], local_sem.at[1]),
         pltpu.make_async_copy(adj_in, aa.at[:, pl.ds(H, nx), rows], local_sem.at[2]),
     ]
-    for copy in locals_:
+    for copy in small + locals_:
         copy.start()
 
     edge = jnp.zeros((PAD, nz), F32)
@@ -83,12 +90,37 @@
 
     lax.fori_loop(0, planes, clear, 0)
 
+    pl.semaphore_wait(barrier, n_space - 1 + n_inj - 1)
+
+    def remote(source, target, send_sem, recv_sem, space, inj):
+        return pltpu.make_async_remote_copy(
+            src_ref=source, dst_ref=target, send_sem=send_sem, recv_sem=recv_sem,
+            device_id=(space, inj), device_id_type=MESH,
+        )
+
+    early = [
+        remote(sig_in.at[pl.ds(nx - H, H)], sigma.at[pl.ds(0, H), rows], halo_send.at[0], halo_recv.at[0], right, my_inj),
+        remote(sig_in.at[pl.ds(0, H)], sigma.at[pl.ds(nx + H, H), rows], halo_send.at[1], halo_recv.at[1], left, my_inj),
+        remote(pot_in.at[:, pl.ds(nx - 3, 3)], pa.at[:, pl.ds(H - 3, 3), rows], halo_send.at[2], halo_recv.at[2], right, my_inj),
+        remote(pot_in.at[:, pl.ds(0, 3)], pa.at[:, pl.ds(nx + H, 3), rows], halo_send.at[3], halo_recv.at[3], left, my_inj),
+    ]
+    late = [
+        remote(adj_in.at[:, pl.ds(nx - H, H)], aa.at[:, pl.ds(0, H), rows], far_send.at[0], far_recv.at[0], right, my_inj),
+        remote(adj_in.at[:, pl.ds(0, H)], aa.at[:, pl.ds(nx + H, H), rows], far_send.at[1], far_recv.at[1], left, my_inj),
+    ]
+    for copy in early:
+        copy.start()
+
+    for copy in small:
+        copy.wait()
     lanes = 4 * blocks
     lane_c = iota((blocks, lanes), 1)
     block_c = lax.rem(lane_c, 2 * blocks) // 2
     field_c = lax.rem(lane_c, 2) + 2 * (lane_c // (2 * blocks))
     row_b = iota((blocks, lanes), 0)
-    owners = jnp.broadcast_to(owner[...].astype(F32), (blocks, lanes))
+    owners = jnp.broadcast_to(owner[...].astype(F32), (blocks, blocks))
+    owners = jnp.where(iota((blocks, blocks), 0) == iota((blocks, blocks), 1), owners, 0.0)
+    owners = jnp.broadcast_to(jnp.sum(owners, axis=1, keepdims=True), (blocks, lanes))
     owner_c = rows_sum(jnp.where(row_b == block_c, owners, 0.0))
     earlier = (owners == owner_c) & (row_b < block_c)
     rank_c = rows_sum(jnp.where(earlier, 1.0, 0.0))
@@ -106,27 +138,6 @@
     packed = jnp.dot(place, data, precision=HIGHEST, preferred_element_type=F32)
     for t in range(n_space):
         send[t] = packed[8 * t : 8 * t + 8]
-
-    pl.semaphore_wait(barrier, n_space - 1 + n_inj - 1)
-
-    def remote(source, target, send_sem, recv_sem, space, inj):
-        return pltpu.make_async_remote_copy(
-            src_ref=source, dst_ref=target, send_sem=send_sem, recv_sem=recv_sem,
-            device_id=(space, inj), device_id_type=MESH,
-        )
-
-    early = [
-        remote(sig_in.at[pl.ds(nx - H, H)], sigma.at[pl.ds(0, H), rows], halo_send.at[0], halo_recv.at[0], right, my_inj),
-        remote(sig_in.at[pl.ds(0, H)], sigma.at[pl.ds(nx + H, H), rows], halo_send.at[1], halo_recv.at[1], left, my_inj),
-        remote(pot_in.at[:, pl.ds(nx - 3, 3)], pa.at[:, pl.ds(H - 3, 3), rows], halo_send.at[2], halo_recv.at[2], right, my_inj),
-        remote(pot_in.at[:, pl.ds(0, 3)], pa.at[:, pl.ds(nx + H, 3), rows], halo_send.at[3], halo_recv.at[3], left, my_inj),
-    ]
-    late = [
-        remote(adj_in.at[:, pl.ds(nx - H, H)], aa.at[:, pl.ds(0, H), rows], far_send.at[0], far_recv.at[0], right, my_inj),
-        remote(adj_in.at[:, pl.ds(0, H)], aa.at[:, pl.ds(nx + H, H), rows], far_send.at[1], far_recv.at[1], left, my_inj),
-    ]
-    for copy in early:
-        copy.start()
 
     def send_block(d, carry):
         to = lax.rem(me + d, n_space)
@@ -258,30 +269,36 @@
         wide_at = within - tall_at * nz + jnp.where(upper, float(nz), 0.0)
         return tall_at, jnp.where(cell < 0.0, -1.0, wide_at)
 
-    def fetch(t, carry):
-        tall_at, wide_at = split_cells(t)
+    def mark(t, carry):
+        _, wide_at = split_cells(t)
         for s in range(2):
             for f in range(2):
                 row = jnp.broadcast_to(wide_at[4 * s + f : 4 * s + f + 1], (wide, elec)).astype(BF16)
                 onehot[t, :, pl.ds((2 * s + f) * elec, elec)] = jnp.where(wide_iota == row, one, none)
-        hot = onehot[t]
-        found = jnp.dot(table[:, :wide], hot, preferred_element_type=F32)
-        found = found + jnp.dot(table[:, wide:], hot, preferred_element_type=F32)
-        out = []
-        for s in range(2):
-            ends = [[], []]
-            for f in range(2):
-                row = tall_at[4 * s + f : 4 * s + f + 1]
-                here = tall_iota == row
+        return carry
+
+    lax.fori_loop(0, n_space, mark, 0)
+
+    def fetch(u, carry):
+        for k in range(group):
+            t = u * group + k
+            tall_at, _ = split_cells(t)
+            hot = onehot[t]
+            found = jnp.dot(table[...], jnp.concatenate([hot, hot], axis=0), preferred_element_type=F32)
+            out = []
+            for s in range(2):
+                ends = [[], []]
+                for f in range(2):
+                    here = tall_iota == tall_at[4 * s + f : 4 * s + f + 1]
+                    for i in range(2):
+                        piece = found[i * tall : (i + 1) * tall, (2 * s + f) * elec : (2 * s + f + 1) * elec]
+                        ends[i].append(rows_sum(jnp.where(here, piece, 0.0)))
                 for i in range(2):
-                    piece = found[i * tall : (i + 1) * tall, (2 * s + f) * elec : (2 * s + f + 1) * elec]
-                    ends[i].append(rows_sum(jnp.where(here, piece, 0.0)))
-            for i in range(2):
-                out.append(ends[i][0] - ends[i][1] - recv[t, pl.ds(4 * s + 2 + i, 1), :])
-        ret_send[t] = jnp.concatenate(out, axis=0)
-        return carry
-
-    lax.fori_loop(0, n_space, fetch, 0)
+                    out.append(ends[i][0] - ends[i][1] - recv[t, pl.ds(4 * s + 2 + i, 1), :])
+            ret_send[t] = jnp.concatenate(out, axis=0)
+        return carry
+
+    lax.fori_loop(0, n_space // group, fetch, 0)
 
     def send_ret(d, carry):
         to = lax.rem(me + d, n_space)
@@ -293,34 +310,36 @@
 
     scat[...] = jnp.zeros_like(scat)
 
-    def spread(t, carry):
-        tall_at, _ = split_cells(t)
-        misfit = ret_send[t]
-        high = misfit.astype(BF16).astype(F32)
-        low = misfit - high
-        columns = [[], []]
-        for s in range(2):
-            for f in range(2):
-                sign = 1.0 if f == 0 else -1.0
-                row = jnp.broadcast_to(tall_at[4 * s + f : 4 * s + f + 1], (tall, elec)).astype(BF16)
-                here = tall_iota16 == row
-                for part, value in enumerate((high, low)):
-                    pieces = []
-                    for i in range(2):
-                        amount = jnp.broadcast_to(sign * value[2 * s + i : 2 * s + i + 1], (tall, elec)).astype(BF16)
-                        pieces.append(jnp.where(here, amount, jnp.zeros((tall, elec), BF16)))
-                    columns[part].append(jnp.concatenate(pieces, axis=0))
-        hot = onehot[t]
-        total = scat[...]
-        for part in range(2):
-            total = total + lax.dot_general(
-                jnp.concatenate(columns[part], axis=1), hot, (((1,), (1,)), ((), ())),
-                preferred_element_type=F32,
-            )
-        scat[...] = total
-        return carry
-
-    lax.fori_loop(0, n_space, spread, 0)
+    def spread(u, carry):
+        amounts, hots = [], []
+        for k in range(group):
+            t = u * group + k
+            tall_at, _ = split_cells(t)
+            misfit = ret_send[t]
+            high = misfit.astype(BF16).astype(F32)
+            low = misfit - high
+            columns = [[], []]
+            for s in range(2):
+                for f in range(2):
+                    sign = 1.0 if f == 0 else -1.0
+                    row = jnp.broadcast_to(tall_at[4 * s + f : 4 * s + f + 1], (tall, elec)).astype(BF16)
+                    here = tall_iota16 == row
+                    for part, value in enumerate((high, low)):
+                        pieces = []
+                        for i in range(2):
+                            amount = jnp.broadcast_to(sign * value[2 * s + i : 2 * s + i + 1], (tall, elec)).astype(BF16)
+                            pieces.append(jnp.where(here, amount, jnp.zeros((tall, elec), BF16)))
+                        columns[part].append(jnp.concatenate(pieces, axis=0))
+            hot = onehot[t]
+            amounts += columns[0] + columns[1]
+            hots += [hot, hot]
+        scat[...] += lax.dot_general(
+            jnp.concatenate(amounts, axis=1), jnp.concatenate(hots, axis=1), (((1,), (1,)), ((), ())),
+            preferred_element_type=F32,
+        )
+        return carry
+
+    lax.fori_loop(0, n_space // group, spread, 0)
     for i in range(2):
         for x in range(nx):
             asrc[i, H + x] = scat[pl.ds(i * tall + (x % half) * ny, ny), pl.ds((x // half) * nz, nz)]
@@ -403,9 +422,8 @@
     blocks, elec = observed.shape[1], observed.shape[3]
     planes, tall_rows = nx + 2 * H, ny + 2 * PAD
     wide, tall = 2 * nz, nx // 2 * ny
-    anywhere = pl.BlockSpec(memory_space=pl.ANY)
+    hbm = pl.BlockSpec(memory_space=pltpu.HBM)
     vmem = pl.BlockSpec(memory_space=pltpu.VMEM)
-    smem = pl.BlockSpec(memory_space=pltpu.SMEM)
     field = pltpu.VMEM((2, planes, tall_rows, nz), F32)
     dma = pltpu.SemaphoreType.DMA
     gradient, residual = pl.pallas_call(
@@ -414,9 +432,14 @@
             jax.ShapeDtypeStruct((nx, ny // n_inj, nz), F32),
             jax.ShapeDtypeStruct((2 * blocks, elec), F32),
         ),
-        in_specs=[anywhere, anywhere, anywhere, smem, vmem, vmem, vmem, vmem],
+        in_specs=[hbm] * 8,
         out_specs=(vmem, vmem),
         scratch_shapes=[
+            pltpu.SMEM((2, 2), jnp.int32),
+            pltpu.VMEM((1, blocks), jnp.int32),
+            pltpu.VMEM((1, blocks), jnp.int32),
+            pltpu.VMEM((2 * blocks, elec), jnp.int32),
+            pltpu.VMEM((2 * blocks, elec), F32),
             pltpu.VMEM((planes, tall_rows, nz), F32),
             field, field, field, field,
             pltpu.VMEM((7, planes, ny, nz), F32),
@@ -432,15 +455,15 @@
             pltpu.VMEM((2 * tall, wide), F32),
             pltpu.VMEM((n_inj, nx, ny // n_inj, nz), F32),
             pltpu.VMEM((n_inj, nx, ny // n_inj, nz), F32),
-            dma((3,)), dma((4,)), dma((4,)), dma((2,)), dma((2,)), dma, dma,
+            dma((8,)), dma((4,)), dma((4,)), dma((2,)), dma((2,)), dma, dma,
             dma, dma, dma((2,)), dma((2,)), dma((2,)), dma((2,)), dma, dma,
         ],
         compiler_params=pltpu.CompilerParams(
-            collective_id=0, has_side_effects=True, vmem_limit_bytes=48 * 1024 * 1024
+            collective_id=0, has_side_effects=True, vmem_limit_bytes=60 * 1024 * 1024
         ),
     )(
         conductivity, start_potential, start_adjoint, inj_cells,
-        owner_tile.reshape(blocks, 1), live_count,
+        owner_tile.reshape(1, blocks), live_count,
         dipole_cells.reshape(2 * blocks, elec), observed.reshape(2 * blocks, elec),
     )
     return gradient, residual.reshape(1, blocks, 2, elec)

time: 76.7 us -> 61.4 us (0.80)
  Pallas kernels: 68.7 us -> 58.6 us
  local copies, waits for them, and re-layouts: 6.98 us -> 1.97 us
    pallas_call x1, Pallas kernels: 68.7 us -> 58.6 us  [body(): pl.pallas_call(functools.partial(kernel, n_space, n_inj, nx, ny, nz, bloc...]
    unnamed x18 -> x4, local copies, waits for them, and re-layouts: 6.9 us -> 1.97 us
where the time goes in v2:
time: 61.4 us; the launch traced here: 61.2 us
  Pallas kernels  58.6 us (95%)
  local copies, waits for them, and re-layouts  1.97 us (3%)
  between operations  0.65 us (1%)
    pallas_call x1, Pallas kernels, body(): pl.pallas_call(functools.partial(kernel, n_space, n_inj, nx, ny, nz, bloc...  58.6 us
    unnamed x4, local copies, waits for them, and re-layouts  1.97 us

profile of v2, /device:TPU:1, one launch (start us, length us, event | category | flops | bytes accessed | tf_op | source)
XLA Modules:
  0.0 61.2 jit_solution(2044331168543245586)
XLA Ops:
  0.6 58.6 %shard_map.95 = (f32[6,8,128]{2,1,0:T(8,128)}, f32[64,128]{1,0:T(8,128)}) custom-call(f32[6,64,128]{2,1,0:T(8,128)} %sig_in.1, f32[2,6,64,128]{3,2,1,0:T(8,128)} %pot_in.1, f32[2,6,64,128]{3,2,1,0:T(8,128)} %adj_in.1, s32[2,2]{1,0:T(2,128)} %inj_in.1, s32[1,32]{1,0:T(1,128)} %bitcast.7, s32[1,32]{1,0:T(1,128)} %live_in.1, s32[64,128]{1,0:T(8,128)} %bitcast.4, ...), custom_call_target="tpu_custom_call" | custom-call | tf_op jit(solution)/shard_map/pallas_call | solution.py:429
  59.2 0.0 copy-start
  59.2 1.4 %copy.12 = f32[6,8,128]{2,1,0:T(8,128)} copy(f32[6,8,128]{2,1,0:T(8,128)} %get-tuple-element.8) | data formatting | bytes 49152
  60.6 0.0 copy-done
  60.6 0.6 %copy.13 = f32[1,32,2,128]{3,2,1,0:T(2,128)} copy(f32[1,32,2,128]{3,2,1,0:T(2,128)S(1)} %bitcast.6) | data formatting | bytes 65536
Async XLA Ops:
  59.2 1.4 %copy-start = (f32[64,128]{1,0:T(8,128)S(1)}, f32[64,128]{1,0:T(8,128)}, u32[]{:S(2)}) copy-start(f32[64,128]{1,0:T(8,128)} %get-tuple-element.5) | copy-start | bytes 98308

commit v3 on v2

--- a/solution.py
+++ b/solution.py
@@ -78,17 +78,10 @@
     for copy in small + locals_:
         copy.start()
 
-    edge = jnp.zeros((PAD, nz), F32)
-
-    def clear(p, carry):
-        for low in (0, PAD + ny):
-            sigma[p, pl.ds(low, PAD), :] = edge
-            for i in range(2):
-                for buf in (pa, pb, aa, ab):
-                    buf[i, p, pl.ds(low, PAD), :] = edge
-        return carry
-
-    lax.fori_loop(0, planes, clear, 0)
+    for low in (0, PAD + ny):
+        sigma[:, pl.ds(low, PAD), :] = jnp.zeros((planes, PAD, nz), F32)
+        for buf in (pa, pb, aa, ab):
+            buf[:, :, pl.ds(low, PAD), :] = jnp.zeros((2, planes, PAD, nz), F32)
 
     pl.semaphore_wait(barrier, n_space - 1 + n_inj - 1)
 
@@ -98,16 +91,24 @@
             device_id=(space, inj), device_id_type=MESH,
         )
 
-    early = [
-        remote(sig_in.at[pl.ds(nx - H, H)], sigma.at[pl.ds(0, H), rows], halo_send.at[0], halo_recv.at[0], right, my_inj),
-        remote(sig_in.at[pl.ds(0, H)], sigma.at[pl.ds(nx + H, H), rows], halo_send.at[1], halo_recv.at[1], left, my_inj),
-        remote(pot_in.at[:, pl.ds(nx - 3, 3)], pa.at[:, pl.ds(H - 3, 3), rows], halo_send.at[2], halo_recv.at[2], right, my_inj),
-        remote(pot_in.at[:, pl.ds(0, 3)], pa.at[:, pl.ds(nx + H, 3), rows], halo_send.at[3], halo_recv.at[3], left, my_inj),
-    ]
+    def pair(source, target, lead, width, send_sems, recv_sems, k):
+        at = (slice(None),) * lead
+        return [
+            remote(
+                source.at[at + (pl.ds(nx - width, width),)], target.at[at + (pl.ds(H - width, width), rows)],
+                send_sems.at[k], recv_sems.at[k], right, my_inj,
+            ),
+            remote(
+                source.at[at + (pl.ds(0, width),)], target.at[at + (pl.ds(nx + H, width), rows)],
+                send_sems.at[k + 1], recv_sems.at[k + 1], left, my_inj,
+            ),
+        ]
+
+    early = pair(sig_in, sigma, 0, 3, halo_send, halo_recv, 0) + pair(pot_in, pa, 1, 3, halo_send, halo_recv, 2)
     late = [
-        remote(adj_in.at[:, pl.ds(nx - H, H)], aa.at[:, pl.ds(0, H), rows], far_send.at[0], far_recv.at[0], right, my_inj),
-        remote(adj_in.at[:, pl.ds(0, H)], aa.at[:, pl.ds(nx + H, H), rows], far_send.at[1], far_recv.at[1], left, my_inj),
-    ]
+        remote(sig_in.at[pl.ds(nx - H, 1)], sigma.at[pl.ds(0, 1), rows], far_send.at[0], far_recv.at[0], right, my_inj),
+        remote(sig_in.at[pl.ds(H - 1, 1)], sigma.at[pl.ds(planes - 1, 1), rows], far_send.at[1], far_recv.at[1], left, my_inj),
+    ] + pair(adj_in, aa, 1, H, far_send, far_recv, 2)
     for copy in early:
         copy.start()
 
@@ -145,96 +146,108 @@
         return carry
 
     lax.fori_loop(1, n_space, send_block, 0)
-    for copy in late:
-        copy.start()
     recv[me] = send[me]
 
     cell_ids = iota((ny, nz), 0) * nz + iota((ny, nz), 1)
 
-    def own_source(p, carry):
+    for p in range(2, planes - 2):
         first = (me * nx - H + p) * (ny * nz)
         for i in range(2):
             plus = jnp.where(cell_ids == inj_cells[i, 0] - first, current_amp, 0.0)
             minus = jnp.where(cell_ids == inj_cells[i, 1] - first, current_amp, 0.0)
             src[i, p] = plus - minus
-        return carry
-
-    lax.fori_loop(0, planes, own_source, 0)
-
-    def no_halo(buf, lead):
-        nothing = jnp.zeros((ny, nz), F32)
-
-        @pl.when(me == 0)
+
+    def beyond(buf, lead, low_side, width):
+        at = (slice(None),) * lead
+        nothing = jnp.zeros((2,) * lead + (width, ny, nz), F32)
+
+        @pl.when(me == (0 if low_side else n_space - 1))
         def _():
-            for p in range(H):
-                for i in range(lead):
-                    if lead == 1:
-                        buf[p, rows, :] = nothing
-                    else:
-                        buf[i, p, rows, :] = nothing
-
-        @pl.when(me == n_space - 1)
-        def _():
-            for p in range(nx + H, planes):
-                for i in range(lead):
-                    if lead == 1:
-                        buf[p, rows, :] = nothing
-                    else:
-                        buf[i, p, rows, :] = nothing
-
-    first_lane = iota((ny, nz), 1) == 0
-    last_lane = iota((ny, nz), 1) == nz - 1
+            buf[at + (pl.ds(H - width if low_side else nx + H, width), rows)] = nothing
+
+    chunk = ny // 2
+
+    def in_chunks(work):
+        def step(q, carry):
+            low = pl.multiple_of(q * chunk, 8)
+            work(low, pl.ds(pl.multiple_of(low + PAD, 8), chunk))
+            return carry
+
+        lax.fori_loop(0, ny // chunk, step, 0)
+
+    first_lane = iota((chunk, nz), 1) == 0
+    last_lane = iota((chunk, nz), 1) == nz - 1
+
+    def next_z(value):
+        return jnp.where(last_lane, 0.0, pltpu.roll(value, nz - 1, 1))
+
+    def last_z(value):
+        return jnp.where(first_lane, 0.0, pltpu.roll(value, 1, 1))
+
+    def faces(which):
+        def work(low, at):
+            for p in which:
+                here = sigma[p, at, :]
+                around = [
+                    sigma[p + 1, at, :], sigma[p - 1, at, :],
+                    sigma[p, pl.ds(low + PAD + 1, chunk), :], sigma[p, pl.ds(low + PAD - 1, chunk), :],
+                    next_z(here), last_z(here),
+                ]
+                around = [0.5 * (here + value) for value in around]
+                diag = around[0] + around[1] + around[2] + around[3] + around[4] + around[5]
+                plane = me * nx - H + p
+                inside = jnp.where((plane >= 0) & (plane < n_space * nx), 1.0, 0.0)
+                inverse = inside / jnp.where(diag > 0.0, diag, 1.0)
+                around[4] = jnp.where(last_lane, 0.0, around[4])
+                around[5] = jnp.where(first_lane, 0.0, around[5])
+                for k in range(6):
+                    coef[k, p, pl.ds(low, chunk), :] = around[k] * inverse
+                coef[6, p, pl.ds(low, chunk), :] = inverse
+
+        in_chunks(work)
+
+    def sweep(source, old, new, which, weight):
+        def work(low, at):
+            for p in which:
+                c = [coef[k, p, pl.ds(low, chunk), :] for k in range(7)]
+                for i in range(2):
+                    here = old[i, p, at, :]
+                    beside = c[0] * old[i, p + 1, at, :] + c[1] * old[i, p - 1, at, :]
+                    beside = beside + (
+                        c[2] * old[i, p, pl.ds(low + PAD + 1, chunk), :] + c[3] * old[i, p, pl.ds(low + PAD - 1, chunk), :]
+                    )
+                    beside = beside + (c[4] * pltpu.roll(here, nz - 1, 1) + c[5] * pltpu.roll(here, 1, 1))
+                    beside = beside + c[6] * source[i, p, pl.ds(low, chunk), :]
+                    new[i, p, at, :] = here + weight * (beside - here)
+
+        in_chunks(work)
+
+    w0, w1, w2 = sweep_weights
+    end = planes - 1
 
     locals_[0].wait()
+    faces(range(H + 1, end - H))
+    locals_[1].wait()
+    sweep(src, pa, pb, range(H + 1, end - H), w0)
+    sweep(src, pb, pa, range(H + 2, end - H - 1), w1)
+
     early[0].wait()
     early[1].wait()
-    no_halo(sigma, 1)
-
-    def faces(p, carry):
-        here = sigma[p, rows, :]
-        zp = jnp.where(last_lane, 0.0, pltpu.roll(here, nz - 1, 1))
-        zm = jnp.where(first_lane, 0.0, pltpu.roll(here, 1, 1))
-        around = [
-            sigma[p + 1, rows, :], sigma[p - 1, rows, :],
-            sigma[p, pl.ds(PAD + 1, ny), :], sigma[p, pl.ds(PAD - 1, ny), :], zp, zm,
-        ]
-        around = [0.5 * (here + value) for value in around]
-        diag = around[0] + around[1] + around[2] + around[3] + around[4] + around[5]
-        plane = me * nx - H + p
-        inside = jnp.where((plane >= 0) & (plane < n_space * nx), 1.0, 0.0)
-        inverse = inside / jnp.where(diag > 0.0, diag, 1.0)
-        around[4] = jnp.where(last_lane, 0.0, around[4])
-        around[5] = jnp.where(first_lane, 0.0, around[5])
-        for k in range(6):
-            coef[k, p] = around[k] * inverse
-        coef[6, p] = inverse
-        return carry
-
-    lax.fori_loop(1, planes - 1, faces, 0)
-
-    def sweep(source, old, new, low, high, weight):
-        def plane(p, carry):
-            c = [coef[k, p] for k in range(7)]
-            for i in range(2):
-                here = old[i, p, rows, :]
-                beside = c[0] * old[i, p + 1, rows, :] + c[1] * old[i, p - 1, rows, :]
-                beside = beside + (
-                    c[2] * old[i, p, pl.ds(PAD + 1, ny), :] + c[3] * old[i, p, pl.ds(PAD - 1, ny), :]
-                )
-                beside = beside + (c[4] * pltpu.roll(here, nz - 1, 1) + c[5] * pltpu.roll(here, 1, 1))
-                beside = beside + c[6] * source[i, p]
-                new[i, p, rows, :] = here + weight * (beside - here)
-            return carry
-
-        lax.fori_loop(low, high, plane, 0)
-
-    locals_[1].wait()
+    beyond(sigma, 0, True, 3)
+    beyond(sigma, 0, False, 3)
+    faces([2, 3, 4, end - 4, end - 3, end - 2])
     early[2].wait()
+    beyond(pa, 1, True, 3)
+    sweep(src, pa, pb, [2, 3, 4], w0)
+    sweep(src, pb, pa, [3, 4, 5], w1)
+    sweep(src, pa, pb, [4, 5, 6], w2)
     early[3].wait()
-    no_halo(pa, 2)
-    sweep(src, pa, pb, 2, planes - 2, sweep_weights[0])
-    sweep(src, pb, pa, 3, planes - 3, sweep_weights[1])
-    sweep(src, pa, pb, H, planes - H, sweep_weights[2])
+    for copy in late:
+        copy.start()
+    beyond(pa, 1, False, 3)
+    sweep(src, pa, pb, [end - 4, end - 3, end - 2], w0)
+    sweep(src, pb, pa, [end - 5, end - 4, end - 3], w1)
+    sweep(src, pa, pb, [end - 6, end - 5, end - 4], w2)
 
     rims = [
         remote(pb.at[:, H + nx - 1, rows], rim.at[0], rim_send.at[0], rim_recv.at[0], right, my_inj),
@@ -351,48 +364,69 @@
         copy.start()
 
     locals_[2].wait()
-    late[0].wait()
-    late[1].wait()
-    no_halo(aa, 2)
+    for copy in late:
+        copy.wait()
+    beyond(sigma, 0, True, H)
+    beyond(sigma, 0, False, H)
+    beyond(aa, 1, True, H)
+    beyond(aa, 1, False, H)
+    faces([1, end - 1])
     for copy in rims:
         copy.wait()
     for i in range(2):
         pb[i, H - 1, rows, :] = jnp.where(me == 0, 0.0, rim[0, i])
         pb[i, H + nx, rows, :] = jnp.where(me == n_space - 1, 0.0, rim[1, i])
-
-    for copy in around:
-        copy.wait()
-    sweep(asrc, aa, ab, 1, planes - 1, sweep_weights[0])
-    sweep(asrc, ab, aa, 2, planes - 2, sweep_weights[1])
-    sweep(asrc, aa, ab, 3, planes - 3, sweep_weights[2])
-
-    def term(x, carry):
-        p = x + H
-        total = jnp.zeros((ny, nz), F32)
-        for i in range(2):
-            here, there = pb[i, p, rows, :], ab[i, p, rows, :]
-            pairs = [
-                (pb[i, p + 1, rows, :], ab[i, p + 1, rows, :]),
-                (pb[i, p - 1, rows, :], ab[i, p - 1, rows, :]),
-                (pb[i, p, pl.ds(PAD + 1, ny), :], ab[i, p, pl.ds(PAD + 1, ny), :]),
-                (pb[i, p, pl.ds(PAD - 1, ny), :], ab[i, p, pl.ds(PAD - 1, ny), :]),
-                tuple(jnp.where(last_lane, 0.0, pltpu.roll(v, nz - 1, 1)) for v in (here, there)),
-                tuple(jnp.where(first_lane, 0.0, pltpu.roll(v, 1, 1)) for v in (here, there)),
-            ]
-            for u, v in pairs:
-                total = total + (here - u) * (there - v)
-        partial[:, x] = (-0.5 * total).reshape(n_inj, ny // n_inj, nz)
-        return carry
-
-    lax.fori_loop(0, nx, term, 0)
-
-    def send_share(d, carry):
-        to = lax.rem(my_inj + d, n_inj)
-        remote(partial.at[to], shares.at[my_inj], share_send, share_recv, me, to).start()
-        return carry
-
-    lax.fori_loop(1, n_inj, send_share, 0)
-    shares[my_inj] = partial[my_inj]
+    sweep(asrc, aa, ab, range(H, H + nx), w0)
+    sweep(asrc, ab, aa, range(H + 1, end - H), w1)
+    sweep(asrc, aa, ab, range(H + 2, end - H - 1), w2)
+
+    def term(side):
+        def work(low, at):
+            for x in range(half):
+                p = H + side * half + x
+                total = jnp.zeros((chunk, nz), F32)
+                for i in range(2):
+                    here, there = pb[i, p, at, :], ab[i, p, at, :]
+                    ahead, behind = pl.ds(low + PAD + 1, chunk), pl.ds(low + PAD - 1, chunk)
+                    pairs = [
+                        (pb[i, p + 1, at, :], ab[i, p + 1, at, :]),
+                        (pb[i, p - 1, at, :], ab[i, p - 1, at, :]),
+                        (pb[i, p, ahead, :], ab[i, p, ahead, :]),
+                        (pb[i, p, behind, :], ab[i, p, behind, :]),
+                        (next_z(here), next_z(there)),
+                        (last_z(here), last_z(there)),
+                    ]
+                    for u, v in pairs:
+                        total = total + (here - u) * (there - v)
+                part = ny // n_inj
+                first = low // part
+                partial[side, pl.ds(first, chunk // part), x] = (-0.5 * total).reshape(chunk // part, part, nz)
+
+        in_chunks(work)
+
+    def send_share(side):
+        def step(d, carry):
+            to = lax.rem(my_inj + d, n_inj)
+            remote(
+                partial.at[side, to], shares.at[side, my_inj], share_send.at[side], share_recv.at[side], me, to
+            ).start()
+            return carry
+
+        lax.fori_loop(1, n_inj, step, 0)
+        shares[side, my_inj] = partial[side, my_inj]
+
+    around[0].wait()
+    sweep(asrc, aa, ab, [1, 2, 3], w0)
+    sweep(asrc, ab, aa, [2, 3, 4], w1)
+    sweep(asrc, aa, ab, [3, 4, 5], w2)
+    term(0)
+    send_share(0)
+    around[1].wait()
+    sweep(asrc, aa, ab, [end - 3, end - 2, end - 1], w0)
+    sweep(asrc, ab, aa, [end - 4, end - 3, end - 2], w1)
+    sweep(asrc, aa, ab, [end - 5, end - 4, end - 3], w2)
+    term(1)
+    send_share(1)
 
     ret_got = pltpu.make_async_copy(ret_recv.at[pl.ds(0, n_space - 1)], ret_recv.at[pl.ds(0, n_space - 1)], ret_recv_sem)
     ret_got.wait()
@@ -402,16 +436,19 @@
     returned = jnp.concatenate([ret_recv[t] for t in range(n_space)], axis=0)
     res_out[...] = jnp.dot(back, returned, precision=HIGHEST, preferred_element_type=F32)
 
-    share_got = pltpu.make_async_copy(shares.at[pl.ds(0, n_inj - 1)], shares.at[pl.ds(0, n_inj - 1)], share_recv)
-    share_got.wait()
-    total = shares[0]
-    for k in range(1, n_inj):
-        total = total + shares[k]
-    grad_out[...] = total
+    for side in range(2):
+        window = shares.at[side, pl.ds(0, n_inj - 1)]
+        pltpu.make_async_copy(window, window, share_recv.at[side]).wait()
+        total = shares[side, 0]
+        for k in range(1, n_inj):
+            total = total + shares[side, k]
+        grad_out[pl.ds(side * half, half)] = total
 
     pltpu.make_async_copy(send.at[pl.ds(0, n_space - 1)], send.at[pl.ds(0, n_space - 1)], block_send).wait()
     pltpu.make_async_copy(ret_send.at[pl.ds(0, n_space - 1)], ret_send.at[pl.ds(0, n_space - 1)], ret_send_sem).wait()
-    pltpu.make_async_copy(partial.at[pl.ds(0, n_inj - 1)], partial.at[pl.ds(0, n_inj - 1)], share_send).wait()
+    for side in range(2):
+        window = partial.at[side, pl.ds(0, n_inj - 1)]
+        pltpu.make_async_copy(window, window, share_send.at[side]).wait()
 
 
 def body(
@@ -453,10 +490,10 @@
             pltpu.VMEM((n_space, wide, 4 * elec), BF16),
             pltpu.VMEM((2 * tall, 2 * wide), BF16),
             pltpu.VMEM((2 * tall, wide), F32),
-            pltpu.VMEM((n_inj, nx, ny // n_inj, nz), F32),
-            pltpu.VMEM((n_inj, nx, ny // n_inj, nz), F32),
-            dma((8,)), dma((4,)), dma((4,)), dma((2,)), dma((2,)), dma, dma,
-            dma, dma, dma((2,)), dma((2,)), dma((2,)), dma((2,)), dma, dma,
+            pltpu.VMEM((2, n_inj, nx // 2, ny // n_inj, nz), F32),
+            pltpu.VMEM((2, n_inj, nx // 2, ny // n_inj, nz), F32),
+            dma((8,)), dma((4,)), dma((4,)), dma((4,)), dma((4,)), dma, dma,
+            dma, dma, dma((2,)), dma((2,)), dma((2,)), dma((2,)), dma((2,)), dma((2,)),
         ],
         compiler_params=pltpu.CompilerParams(
             collective_id=0, has_side_effects=True, vmem_limit_bytes=60 * 1024 * 1024

time: 61.4 us -> 55.2 us (0.90)
  Pallas kernels: 58.6 us -> 52.5 us
    pallas_call x1, Pallas kernels: 58.6 us -> 52.5 us  [body(): pl.pallas_call(functools.partial(kernel, n_space, n_inj, nx, ny, nz, bloc...]
where the time goes in v3:
time: 55.2 us; the launch traced here: 55.1 us
  Pallas kernels  52.5 us (95%)
  local copies, waits for them, and re-layouts  1.97 us (4%)
  between operations  0.65 us (1%)
    pallas_call x1, Pallas kernels, body(): pl.pallas_call(functools.partial(kernel, n_space, n_inj, nx, ny, nz, bloc...  52.5 us
    unnamed x4, local copies, waits for them, and re-layouts  1.97 us

profile of v3, /device:TPU:1, one launch (start us, length us, event | category | flops | bytes accessed | tf_op | source)
XLA Modules:
  0.0 55.1 jit_solution(1760643077873352772)
XLA Ops:
  0.6 52.5 %shard_map.95 = (f32[6,8,128]{2,1,0:T(8,128)}, f32[64,128]{1,0:T(8,128)}) custom-call(f32[6,64,128]{2,1,0:T(8,128)} %sig_in.1, f32[2,6,64,128]{3,2,1,0:T(8,128)} %pot_in.1, f32[2,6,64,128]{3,2,1,0:T(8,128)} %adj_in.1, s32[2,2]{1,0:T(2,128)} %inj_in.1, s32[1,32]{1,0:T(1,128)} %bitcast.7, s32[1,32]{1,0:T(1,128)} %live_in.1, s32[64,128]{1,0:T(8,128)} %bitcast.4, ...), custom_call_target="tpu_custom_call" | custom-call | tf_op jit(solution)/shard_map/pallas_call | solution.py:466
  53.1 0.0 copy-start
  53.1 1.4 %copy.12 = f32[6,8,128]{2,1,0:T(8,128)} copy(f32[6,8,128]{2,1,0:T(8,128)} %get-tuple-element.8) | data formatting | bytes 49152
  54.5 0.0 copy-done
  54.5 0.6 %copy.13 = f32[1,32,2,128]{3,2,1,0:T(2,128)} copy(f32[1,32,2,128]{3,2,1,0:T(2,128)S(1)} %bitcast.6) | data formatting | bytes 65536
Async XLA Ops:
  53.1 1.4 %copy-start = (f32[64,128]{1,0:T(8,128)S(1)}, f32[64,128]{1,0:T(8,128)}, u32[]{:S(2)}) copy-start(f32[64,128]{1,0:T(8,128)} %get-tuple-element.5) | copy-start | bytes 98308

commit v4 on v3

--- a/solution.py
+++ b/solution.py
@@ -49,19 +49,24 @@
     tall = half * ny
     wide = 2 * nz
     half_cells = float(half * ny * nz)
-    group = math.gcd(n_space, 8)
+    group = math.gcd(n_space, 16)
 
     barrier = pltpu.get_barrier_semaphore()
 
-    def greet(d, carry):
-        pl.semaphore_signal(barrier, inc=1, device_id=(lax.rem(me + d, n_space), my_inj), device_id_type=MESH)
+    def greet(to):
+        pl.semaphore_signal(barrier, inc=1, device_id=to, device_id_type=MESH)
+
+    def greet_space(d, carry):
+        greet((lax.rem(me + d, n_space), my_inj))
         return carry
 
     def greet_inj(d, carry):
-        pl.semaphore_signal(barrier, inc=1, device_id=(me, lax.rem(my_inj + d, n_inj)), device_id_type=MESH)
+        greet((me, lax.rem(my_inj + d, n_inj)))
         return carry
 
-    lax.fori_loop(1, n_space, greet, 0)
+    greet((left, my_inj))
+    greet((right, my_inj))
+    lax.fori_loop(2, n_space - 1, greet_space, 0)
     lax.fori_loop(1, n_inj, greet_inj, 0)
 
     small = [
@@ -92,24 +97,24 @@
         )
 
     def pair(source, target, lead, width, send_sems, recv_sems, k):
-        at = (slice(None),) * lead
         return [
             remote(
-                source.at[at + (pl.ds(nx - width, width),)], target.at[at + (pl.ds(H - width, width), rows)],
+                source.at[lead + (pl.ds(nx - width, width),)], target.at[lead + (pl.ds(H - width, width), rows)],
                 send_sems.at[k], recv_sems.at[k], right, my_inj,
             ),
             remote(
-                source.at[at + (pl.ds(0, width),)], target.at[at + (pl.ds(nx + H, width), rows)],
+                source.at[lead + (pl.ds(0, width),)], target.at[lead + (pl.ds(nx + H, width), rows)],
                 send_sems.at[k + 1], recv_sems.at[k + 1], left, my_inj,
             ),
         ]
 
-    early = pair(sig_in, sigma, 0, 3, halo_send, halo_recv, 0) + pair(pot_in, pa, 1, 3, halo_send, halo_recv, 2)
+    early = pair(sig_in, sigma, (), 3, halo_send, halo_recv, 0)
+    near = [pair(pot_in, pa, (i,), 3, halo_send, halo_recv, 2 + 2 * i) for i in range(2)]
     late = [
         remote(sig_in.at[pl.ds(nx - H, 1)], sigma.at[pl.ds(0, 1), rows], far_send.at[0], far_recv.at[0], right, my_inj),
         remote(sig_in.at[pl.ds(H - 1, 1)], sigma.at[pl.ds(planes - 1, 1), rows], far_send.at[1], far_recv.at[1], left, my_inj),
-    ] + pair(adj_in, aa, 1, H, far_send, far_recv, 2)
-    for copy in early:
+    ] + pair(adj_in, aa, (slice(None),), H, far_send, far_recv, 2)
+    for copy in early + near[0]:
         copy.start()
 
     for copy in small:
@@ -146,6 +151,8 @@
         return carry
 
     lax.fori_loop(1, n_space, send_block, 0)
+    for copy in near[1]:
+        copy.start()
     recv[me] = send[me]
 
     cell_ids = iota((ny, nz), 0) * nz + iota((ny, nz), 1)
@@ -158,12 +165,11 @@
             src[i, p] = plus - minus
 
     def beyond(buf, lead, low_side, width):
-        at = (slice(None),) * lead
-        nothing = jnp.zeros((2,) * lead + (width, ny, nz), F32)
+        nothing = jnp.zeros((width, ny, nz), F32)
 
         @pl.when(me == (0 if low_side else n_space - 1))
         def _():
-            buf[at + (pl.ds(H - width if low_side else nx + H, width), rows)] = nothing
+            buf[lead + (pl.ds(H - width if low_side else nx + H, width), rows)] = nothing
 
     chunk = ny // 2
 
@@ -206,19 +212,18 @@
 
         in_chunks(work)
 
-    def sweep(source, old, new, which, weight):
+    def sweep(i, source, old, new, which, weight):
         def work(low, at):
             for p in which:
                 c = [coef[k, p, pl.ds(low, chunk), :] for k in range(7)]
-                for i in range(2):
-                    here = old[i, p, at, :]
-                    beside = c[0] * old[i, p + 1, at, :] + c[1] * old[i, p - 1, at, :]
-                    beside = beside + (
-                        c[2] * old[i, p, pl.ds(low + PAD + 1, chunk), :] + c[3] * old[i, p, pl.ds(low + PAD - 1, chunk), :]
-                    )
-                    beside = beside + (c[4] * pltpu.roll(here, nz - 1, 1) + c[5] * pltpu.roll(here, 1, 1))
-                    beside = beside + c[6] * source[i, p, pl.ds(low, chunk), :]
-                    new[i, p, at, :] = here + weight * (beside - here)
+                here = old[i, p, at, :]
+                beside = c[0] * old[i, p + 1, at, :] + c[1] * old[i, p - 1, at, :]
+                beside = beside + (
+                    c[2] * old[i, p, pl.ds(low + PAD + 1, chunk), :] + c[3] * old[i, p, pl.ds(low + PAD - 1, chunk), :]
+                )
+                beside = beside + (c[4] * pltpu.roll(here, nz - 1, 1) + c[5] * pltpu.roll(here, 1, 1))
+                beside = beside + c[6] * source[i, p, pl.ds(low, chunk), :]
+                new[i, p, at, :] = here + weight * (beside - here)
 
         in_chunks(work)
 
@@ -228,45 +233,31 @@
     locals_[0].wait()
     faces(range(H + 1, end - H))
     locals_[1].wait()
-    sweep(src, pa, pb, range(H + 1, end - H), w0)
-    sweep(src, pb, pa, range(H + 2, end - H - 1), w1)
-
-    early[0].wait()
-    early[1].wait()
-    beyond(sigma, 0, True, 3)
-    beyond(sigma, 0, False, 3)
+    for i in range(2):
+        sweep(i, src, pa, pb, range(H + 1, end - H), w0)
+        sweep(i, src, pb, pa, range(H + 2, end - H - 1), w1)
+
+    for copy in early:
+        copy.wait()
+    beyond(sigma, (), True, 3)
+    beyond(sigma, (), False, 3)
     faces([2, 3, 4, end - 4, end - 3, end - 2])
-    early[2].wait()
-    beyond(pa, 1, True, 3)
-    sweep(src, pa, pb, [2, 3, 4], w0)
-    sweep(src, pb, pa, [3, 4, 5], w1)
-    sweep(src, pa, pb, [4, 5, 6], w2)
-    early[3].wait()
-    for copy in late:
-        copy.start()
-    beyond(pa, 1, False, 3)
-    sweep(src, pa, pb, [end - 4, end - 3, end - 2], w0)
-    sweep(src, pb, pa, [end - 5, end - 4, end - 3], w1)
-    sweep(src, pa, pb, [end - 6, end - 5, end - 4], w2)
-
-    rims = [
-        remote(pb.at[:, H + nx - 1, rows], rim.at[0], rim_send.at[0], rim_recv.at[0], right, my_inj),
-        remote(pb.at[:, H, rows], rim.at[1], rim_send.at[1], rim_recv.at[1], left, my_inj),
-    ]
-    for copy in rims:
-        copy.start()
-
-    for i in range(2):
+
+    def finish_potential(i):
+        for copy in near[i]:
+            copy.wait()
+        beyond(pa, (i,), True, 3)
+        beyond(pa, (i,), False, 3)
+        sweep(i, src, pa, pb, [2, 3, 4, end - 4, end - 3, end - 2], w0)
+        sweep(i, src, pb, pa, [3, 4, 5, end - 5, end - 4, end - 3], w1)
+        sweep(i, src, pa, pb, range(H, H + nx), w2)
         for x in range(nx):
             value = pb[i, H + x, rows, :]
             high = value.astype(BF16)
             low = (value - high.astype(F32)).astype(BF16)
-            at = (pl.ds(i * tall + (x % half) * ny, ny))
-            table[at, pl.ds((x // half) * nz, nz)] = high
-            table[at, pl.ds(wide + (x // half) * nz, nz)] = low
-
-    got = pltpu.make_async_copy(recv.at[pl.ds(0, n_space - 1)], recv.at[pl.ds(0, n_space - 1)], block_recv)
-    got.wait()
+            first, columns = (x % half) * ny, pl.ds((x // half) * nz, nz)
+            table[i, pl.ds(first, ny), columns] = high
+            table[i, pl.ds(tall + first, ny), columns] = low
 
     wide_iota = iota((wide, elec), 0).astype(F32).astype(BF16)
     tall_iota = iota((tall, elec), 0).astype(F32)
@@ -290,28 +281,90 @@
                 onehot[t, :, pl.ds((2 * s + f) * elec, elec)] = jnp.where(wide_iota == row, one, none)
         return carry
 
+    def fetch(i):
+        def step(u, carry):
+            for k in range(group):
+                t = u * group + k
+                tall_at, _ = split_cells(t)
+                found = jnp.dot(table[i], onehot[t], preferred_element_type=F32)
+                for s in range(2):
+                    ends = []
+                    for f in range(2):
+                        here = tall_iota == tall_at[4 * s + f : 4 * s + f + 1]
+                        at = slice((2 * s + f) * elec, (2 * s + f + 1) * elec)
+                        ends.append(rows_sum(jnp.where(here, found[:tall, at] + found[tall:, at], 0.0)))
+                    ret_send[t, pl.ds(2 * s + i, 1), :] = ends[0] - ends[1] - recv[t, pl.ds(4 * s + 2 + i, 1), :]
+            return carry
+
+        lax.fori_loop(0, n_space // group, step, 0)
+
+    def spread(i):
+        scat[...] = jnp.zeros_like(scat)
+
+        def step(u, carry):
+            amounts, hots = [], []
+            for k in range(group):
+                t = u * group + k
+                tall_at, _ = split_cells(t)
+                misfit = ret_send[t]
+                high = misfit.astype(BF16).astype(F32)
+                for s in range(2):
+                    for f in range(2):
+                        sign = 1.0 if f == 0 else -1.0
+                        row = jnp.broadcast_to(tall_at[4 * s + f : 4 * s + f + 1], (tall, elec)).astype(BF16)
+                        here = tall_iota16 == row
+                        pieces = []
+                        for value in (high, misfit - high):
+                            amount = jnp.broadcast_to(sign * value[2 * s + i : 2 * s + i + 1], (tall, elec)).astype(BF16)
+                            pieces.append(jnp.where(here, amount, jnp.zeros((tall, elec), BF16)))
+                        amounts.append(jnp.concatenate(pieces, axis=0))
+                hots.append(onehot[t])
+            scat[...] += lax.dot_general(
+                jnp.concatenate(amounts, axis=1), jnp.concatenate(hots, axis=1), (((1,), (1,)), ((), ())),
+                preferred_element_type=F32,
+            )
+            return carry
+
+        lax.fori_loop(0, n_space // group, step, 0)
+        for x in range(nx):
+            first, columns = (x % half) * ny, pl.ds((x // half) * nz, nz)
+            asrc[i, H + x] = scat[pl.ds(first, ny), columns] + scat[pl.ds(tall + first, ny), columns]
+
+    rims = [
+        [
+            remote(pb.at[i, H + nx - 1, rows], rim.at[0, i], rim_send.at[2 * i], rim_recv.at[2 * i], right, my_inj),
+            remote(pb.at[i, H, rows], rim.at[1, i], rim_send.at[2 * i + 1], rim_recv.at[2 * i + 1], left, my_inj),
+        ]
+        for i in range(2)
+    ]
+    around = [
+        [
+            remote(
+                asrc.at[i, pl.ds(H + nx - 3, 3)], asrc.at[i, pl.ds(1, 3)],
+                asrc_send.at[2 * i], asrc_recv.at[2 * i], right, my_inj,
+            ),
+            remote(
+                asrc.at[i, pl.ds(H, 3)], asrc.at[i, pl.ds(H + nx, 3)],
+                asrc_send.at[2 * i + 1], asrc_recv.at[2 * i + 1], left, my_inj,
+            ),
+        ]
+        for i in range(2)
+    ]
+
+    finish_potential(0)
+    for copy in rims[0]:
+        copy.start()
+    got = pltpu.make_async_copy(recv.at[pl.ds(0, n_space - 1)], recv.at[pl.ds(0, n_space - 1)], block_recv)
+    got.wait()
     lax.fori_loop(0, n_space, mark, 0)
-
-    def fetch(u, carry):
-        for k in range(group):
-            t = u * group + k
-            tall_at, _ = split_cells(t)
-            hot = onehot[t]
-            found = jnp.dot(table[...], jnp.concatenate([hot, hot], axis=0), preferred_element_type=F32)
-            out = []
-            for s in range(2):
-                ends = [[], []]
-                for f in range(2):
-                    here = tall_iota == tall_at[4 * s + f : 4 * s + f + 1]
-                    for i in range(2):
-                        piece = found[i * tall : (i + 1) * tall, (2 * s + f) * elec : (2 * s + f + 1) * elec]
-                        ends[i].append(rows_sum(jnp.where(here, piece, 0.0)))
-                for i in range(2):
-                    out.append(ends[i][0] - ends[i][1] - recv[t, pl.ds(4 * s + 2 + i, 1), :])
-            ret_send[t] = jnp.concatenate(out, axis=0)
-        return carry
-
-    lax.fori_loop(0, n_space // group, fetch, 0)
+    fetch(0)
+    finish_potential(1)
+    for copy in late + rims[1]:
+        copy.start()
+    spread(0)
+    for copy in around[0]:
+        copy.start()
+    fetch(1)
 
     def send_ret(d, carry):
         to = lax.rem(me + d, n_space)
@@ -321,86 +374,54 @@
     lax.fori_loop(1, n_space, send_ret, 0)
     ret_recv[me] = ret_send[me]
 
-    scat[...] = jnp.zeros_like(scat)
-
-    def spread(u, carry):
-        amounts, hots = [], []
-        for k in range(group):
-            t = u * group + k
-            tall_at, _ = split_cells(t)
-            misfit = ret_send[t]
-            high = misfit.astype(BF16).astype(F32)
-            low = misfit - high
-            columns = [[], []]
-            for s in range(2):
-                for f in range(2):
-                    sign = 1.0 if f == 0 else -1.0
-                    row = jnp.broadcast_to(tall_at[4 * s + f : 4 * s + f + 1], (tall, elec)).astype(BF16)
-                    here = tall_iota16 == row
-                    for part, value in enumerate((high, low)):
-                        pieces = []
-                        for i in range(2):
-                            amount = jnp.broadcast_to(sign * value[2 * s + i : 2 * s + i + 1], (tall, elec)).astype(BF16)
-                            pieces.append(jnp.where(here, amount, jnp.zeros((tall, elec), BF16)))
-                        columns[part].append(jnp.concatenate(pieces, axis=0))
-            hot = onehot[t]
-            amounts += columns[0] + columns[1]
-            hots += [hot, hot]
-        scat[...] += lax.dot_general(
-            jnp.concatenate(amounts, axis=1), jnp.concatenate(hots, axis=1), (((1,), (1,)), ((), ())),
-            preferred_element_type=F32,
-        )
-        return carry
-
-    lax.fori_loop(0, n_space // group, spread, 0)
-    for i in range(2):
-        for x in range(nx):
-            asrc[i, H + x] = scat[pl.ds(i * tall + (x % half) * ny, ny), pl.ds((x // half) * nz, nz)]
-    around = [
-        remote(asrc.at[:, pl.ds(H + nx - 3, 3)], asrc.at[:, pl.ds(1, 3)], asrc_send.at[0], asrc_recv.at[0], right, my_inj),
-        remote(asrc.at[:, pl.ds(H, 3)], asrc.at[:, pl.ds(H + nx, 3)], asrc_send.at[1], asrc_recv.at[1], left, my_inj),
-    ]
-    for copy in around:
+    spread(1)
+    for copy in around[1]:
         copy.start()
 
     locals_[2].wait()
     for copy in late:
         copy.wait()
-    beyond(sigma, 0, True, H)
-    beyond(sigma, 0, False, H)
-    beyond(aa, 1, True, H)
-    beyond(aa, 1, False, H)
+    for low_side in (True, False):
+        beyond(sigma, (), low_side, H)
+        for i in range(2):
+            beyond(aa, (i,), low_side, H)
     faces([1, end - 1])
-    for copy in rims:
-        copy.wait()
     for i in range(2):
+        for copy in rims[i]:
+            copy.wait()
         pb[i, H - 1, rows, :] = jnp.where(me == 0, 0.0, rim[0, i])
         pb[i, H + nx, rows, :] = jnp.where(me == n_space - 1, 0.0, rim[1, i])
-    sweep(asrc, aa, ab, range(H, H + nx), w0)
-    sweep(asrc, ab, aa, range(H + 1, end - H), w1)
-    sweep(asrc, aa, ab, range(H + 2, end - H - 1), w2)
-
-    def term(side):
+
+    for copy in around[0]:
+        copy.wait()
+    sweep(0, asrc, aa, ab, range(1, planes - 1), w0)
+    sweep(0, asrc, ab, aa, range(2, planes - 2), w1)
+    sweep(0, asrc, aa, ab, range(3, planes - 3), w2)
+    sweep(1, asrc, aa, ab, range(H, H + nx), w0)
+    sweep(1, asrc, ab, aa, range(H + 1, end - H), w1)
+    sweep(1, asrc, aa, ab, range(H + 2, end - H - 1), w2)
+
+    def term(i, side):
         def work(low, at):
+            part = ny // n_inj
+            where = pl.ds(low // part, chunk // part)
             for x in range(half):
                 p = H + side * half + x
+                here, there = pb[i, p, at, :], ab[i, p, at, :]
+                ahead, behind = pl.ds(low + PAD + 1, chunk), pl.ds(low + PAD - 1, chunk)
+                pairs = [
+                    (pb[i, p + 1, at, :], ab[i, p + 1, at, :]),
+                    (pb[i, p - 1, at, :], ab[i, p - 1, at, :]),
+                    (pb[i, p, ahead, :], ab[i, p, ahead, :]),
+                    (pb[i, p, behind, :], ab[i, p, behind, :]),
+                    (next_z(here), next_z(there)),
+                    (last_z(here), last_z(there)),
+                ]
                 total = jnp.zeros((chunk, nz), F32)
-                for i in range(2):
-                    here, there = pb[i, p, at, :], ab[i, p, at, :]
-                    ahead, behind = pl.ds(low + PAD + 1, chunk), pl.ds(low + PAD - 1, chunk)
-                    pairs = [
-                        (pb[i, p + 1, at, :], ab[i, p + 1, at, :]),
-                        (pb[i, p - 1, at, :], ab[i, p - 1, at, :]),
-                        (pb[i, p, ahead, :], ab[i, p, ahead, :]),
-                        (pb[i, p, behind, :], ab[i, p, behind, :]),
-                        (next_z(here), next_z(there)),
-                        (last_z(here), last_z(there)),
-                    ]
-                    for u, v in pairs:
-                        total = total + (here - u) * (there - v)
-                part = ny // n_inj
-                first = low // part
-                partial[side, pl.ds(first, chunk // part), x] = (-0.5 * total).reshape(chunk // part, part, nz)
+                for u, v in pairs:
+                    total = total + (here - u) * (there - v)
+                total = (-0.5 * total).reshape(chunk // part, part, nz)
+                partial[side, where, x] = total if i == 0 else partial[side, where, x] + total
 
         in_chunks(work)
 
@@ -415,17 +436,19 @@
         lax.fori_loop(1, n_inj, step, 0)
         shares[side, my_inj] = partial[side, my_inj]
 
-    around[0].wait()
-    sweep(asrc, aa, ab, [1, 2, 3], w0)
-    sweep(asrc, ab, aa, [2, 3, 4], w1)
-    sweep(asrc, aa, ab, [3, 4, 5], w2)
-    term(0)
+    term(0, 0)
+    term(0, 1)
+    around[1][0].wait()
+    sweep(1, asrc, aa, ab, [1, 2, 3], w0)
+    sweep(1, asrc, ab, aa, [2, 3, 4], w1)
+    sweep(1, asrc, aa, ab, [3, 4, 5], w2)
+    term(1, 0)
     send_share(0)
-    around[1].wait()
-    sweep(asrc, aa, ab, [end - 3, end - 2, end - 1], w0)
-    sweep(asrc, ab, aa, [end - 4, end - 3, end - 2], w1)
-    sweep(asrc, aa, ab, [end - 5, end - 4, end - 3], w2)
-    term(1)
+    around[1][1].wait()
+    sweep(1, asrc, aa, ab, [end - 3, end - 2, end - 1], w0)
+    sweep(1, asrc, ab, aa, [end - 4, end - 3, end - 2], w1)
+    sweep(1, asrc, aa, ab, [end - 5, end - 4, end - 3], w2)
+    term(1, 1)
     send_share(1)
 
     ret_got = pltpu.make_async_copy(ret_recv.at[pl.ds(0, n_space - 1)], ret_recv.at[pl.ds(0, n_space - 1)], ret_recv_sem)
@@ -488,12 +511,12 @@
             pltpu.VMEM((n_space, 4, elec), F32),
             pltpu.VMEM((2, 2, ny, nz), F32),
             pltpu.VMEM((n_space, wide, 4 * elec), BF16),
-            pltpu.VMEM((2 * tall, 2 * wide), BF16),
+            pltpu.VMEM((2, 2 * tall, wide), BF16),
             pltpu.VMEM((2 * tall, wide), F32),
             pltpu.VMEM((2, n_inj, nx // 2, ny // n_inj, nz), F32),
             pltpu.VMEM((2, n_inj, nx // 2, ny // n_inj, nz), F32),
-            dma((8,)), dma((4,)), dma((4,)), dma((4,)), dma((4,)), dma, dma,
-            dma, dma, dma((2,)), dma((2,)), dma((2,)), dma((2,)), dma((2,)), dma((2,)),
+            dma((8,)), dma((6,)), dma((6,)), dma((4,)), dma((4,)), dma, dma,
+            dma, dma, dma((4,)), dma((4,)), dma((4,)), dma((4,)), dma((2,)), dma((2,)),
         ],
         compiler_params=pltpu.CompilerParams(
             collective_id=0, has_side_effects=True, vmem_limit_bytes=60 * 1024 * 1024

time: 55.2 us -> 51.3 us (0.929); the launches traced: 55.1 us -> 50.5 us
  Pallas kernels: 52.5 us -> 47.8 us
    pallas_call x1, Pallas kernels: 52.5 us -> 47.8 us  [body(): pl.pallas_call(functools.partial(kernel, n_space, n_inj, nx, ny, nz, bloc...]
where the time goes in v4:
time: 51.3 us; the launch traced here: 50.5 us
  Pallas kernels  47.8 us (93%)
  local copies, waits for them, and re-layouts  1.97 us (4%)
  between operations  0.65 us (1%)
    pallas_call x1, Pallas kernels, body(): pl.pallas_call(functools.partial(kernel, n_space, n_inj, nx, ny, nz, bloc...  47.8 us
    unnamed x4, local copies, waits for them, and re-layouts  1.97 us

profile of v4, /device:TPU:1, one launch (start us, length us, event | category | flops | bytes accessed | tf_op | source)
XLA Modules:
  0.0 50.5 jit_solution(17197318985099297417)
XLA Ops:
  0.6 47.8 %shard_map.95 = (f32[6,8,128]{2,1,0:T(8,128)}, f32[64,128]{1,0:T(8,128)}) custom-call(f32[6,64,128]{2,1,0:T(8,128)} %sig_in.1, f32[2,6,64,128]{3,2,1,0:T(8,128)} %pot_in.1, f32[2,6,64,128]{3,2,1,0:T(8,128)} %adj_in.1, s32[2,2]{1,0:T(2,128)} %inj_in.1, s32[1,32]{1,0:T(1,128)} %bitcast.7, s32[1,32]{1,0:T(1,128)} %live_in.1, s32[64,128]{1,0:T(8,128)} %bitcast.4, ...), custom_call_target="tpu_custom_call" | custom-call | tf_op jit(solution)/shard_map/pallas_call | solution.py:489
  48.5 0.0 copy-start
  48.5 1.4 %copy.12 = f32[6,8,128]{2,1,0:T(8,128)} copy(f32[6,8,128]{2,1,0:T(8,128)} %get-tuple-element.8) | data formatting | bytes 49152
  49.8 0.0 copy-done
  49.9 0.6 %copy.13 = f32[1,32,2,128]{3,2,1,0:T(2,128)} copy(f32[1,32,2,128]{3,2,1,0:T(2,128)S(1)} %bitcast.6) | data formatting | bytes 65536
Async XLA Ops:
  48.5 1.4 %copy-start = (f32[64,128]{1,0:T(8,128)S(1)}, f32[64,128]{1,0:T(8,128)}, u32[]{:S(2)}) copy-start(f32[64,128]{1,0:T(8,128)} %get-tuple-element.5) | copy-start | bytes 98308

commit v5 on v4

--- a/solution.py
+++ b/solution.py
@@ -33,9 +33,9 @@
 def kernel(
     n_space, n_inj, nx, ny, nz, blocks,
     sig_in, pot_in, adj_in, inj_in, owner_in, live_in, cells_in, observed_in,
-    grad_out, res_out,
+    shares, res_out,
     inj_cells, owner, live, cells, observed, sigma, pa, pb, aa, ab, coef, src, asrc, send, recv, ret_send, ret_recv,
-    rim, onehot, table, scat, partial, shares,
+    rim, onehot, table, scat, partial, res,
     local_sem, halo_send, halo_recv, far_send, far_recv, block_send, block_recv,
     ret_send_sem, ret_recv_sem, rim_send, rim_recv, asrc_send, asrc_recv, share_send, share_recv,
 ):
@@ -425,6 +425,9 @@
 
         in_chunks(work)
 
+    def own_share(side):
+        return pltpu.make_async_copy(partial.at[side, my_inj], shares.at[side, my_inj], local_sem.at[8 + side])
+
     def send_share(side):
         def step(d, carry):
             to = lax.rem(my_inj + d, n_inj)
@@ -434,7 +437,7 @@
             return carry
 
         lax.fori_loop(1, n_inj, step, 0)
-        shares[side, my_inj] = partial[side, my_inj]
+        own_share(side).start()
 
     term(0, 0)
     term(0, 1)
@@ -457,21 +460,32 @@
     back = jnp.where(iota((n_space * 4, lanes), 0).astype(F32) == slot_c * 2.0 + lane_j, 1.0, 0.0)
     back = jnp.transpose(back)[: 2 * blocks]
     returned = jnp.concatenate([ret_recv[t] for t in range(n_space)], axis=0)
-    res_out[...] = jnp.dot(back, returned, precision=HIGHEST, preferred_element_type=F32)
-
-    for side in range(2):
-        window = shares.at[side, pl.ds(0, n_inj - 1)]
-        pltpu.make_async_copy(window, window, share_recv.at[side]).wait()
-        total = shares[side, 0]
-        for k in range(1, n_inj):
-            total = total + shares[side, k]
-        grad_out[pl.ds(side * half, half)] = total
+    res[...] = jnp.dot(back, returned, precision=HIGHEST, preferred_element_type=F32)
+    res_copy = pltpu.make_async_copy(res, res_out, local_sem.at[10])
+    res_copy.start()
 
     pltpu.make_async_copy(send.at[pl.ds(0, n_space - 1)], send.at[pl.ds(0, n_space - 1)], block_send).wait()
     pltpu.make_async_copy(ret_send.at[pl.ds(0, n_space - 1)], ret_send.at[pl.ds(0, n_space - 1)], ret_send_sem).wait()
     for side in range(2):
         window = partial.at[side, pl.ds(0, n_inj - 1)]
         pltpu.make_async_copy(window, window, share_send.at[side]).wait()
+        own_share(side).wait()
+    res_copy.wait()
+    for side in range(2):
+        window = shares.at[side, pl.ds(0, n_inj - 1)]
+        pltpu.make_async_copy(window, window, share_recv.at[side]).wait()
+
+
+def gather_up(shares, res_in, gradient, res_out, sem):
+    copy = pltpu.make_async_copy(res_in, res_out, sem)
+    copy.start()
+    n_inj, half = shares.shape[1], shares.shape[2]
+    for side in range(2):
+        total = shares[side, 0]
+        for k in range(1, n_inj):
+            total = total + shares[side, k]
+        gradient[pl.ds(side * half, half)] = total
+    copy.wait()
 
 
 def body(
@@ -486,14 +500,14 @@
     vmem = pl.BlockSpec(memory_space=pltpu.VMEM)
     field = pltpu.VMEM((2, planes, tall_rows, nz), F32)
     dma = pltpu.SemaphoreType.DMA
-    gradient, residual = pl.pallas_call(
+    shares, residual = pl.pallas_call(
         functools.partial(kernel, n_space, n_inj, nx, ny, nz, blocks),
         out_shape=(
-            jax.ShapeDtypeStruct((nx, ny // n_inj, nz), F32),
+            jax.ShapeDtypeStruct((2, n_inj, nx // 2, ny // n_inj, nz), F32),
             jax.ShapeDtypeStruct((2 * blocks, elec), F32),
         ),
         in_specs=[hbm] * 8,
-        out_specs=(vmem, vmem),
+        out_specs=(hbm, hbm),
         scratch_shapes=[
             pltpu.SMEM((2, 2), jnp.int32),
             pltpu.VMEM((1, blocks), jnp.int32),
@@ -514,8 +528,8 @@
             pltpu.VMEM((2, 2 * tall, wide), BF16),
             pltpu.VMEM((2 * tall, wide), F32),
             pltpu.VMEM((2, n_inj, nx // 2, ny // n_inj, nz), F32),
-            pltpu.VMEM((2, n_inj, nx // 2, ny // n_inj, nz), F32),
-            dma((8,)), dma((6,)), dma((6,)), dma((4,)), dma((4,)), dma, dma,
+            pltpu.VMEM((2 * blocks, elec), F32),
+            dma((11,)), dma((6,)), dma((6,)), dma((4,)), dma((4,)), dma, dma,
             dma, dma, dma((4,)), dma((4,)), dma((4,)), dma((4,)), dma((2,)), dma((2,)),
         ],
         compiler_params=pltpu.CompilerParams(
@@ -526,6 +540,17 @@
         owner_tile.reshape(1, blocks), live_count,
         dipole_cells.reshape(2 * blocks, elec), observed.reshape(2 * blocks, elec),
     )
+    gradient, residual = pl.pallas_call(
+        gather_up,
+        out_shape=(
+            jax.ShapeDtypeStruct((nx, ny // n_inj, nz), F32),
+            jax.ShapeDtypeStruct((2 * blocks, elec), F32),
+        ),
+        in_specs=[vmem, hbm],
+        out_specs=(vmem, hbm),
+        scratch_shapes=[dma],
+        compiler_params=pltpu.CompilerParams(vmem_limit_bytes=60 * 1024 * 1024),
+    )(shares, residual)
     return gradient, residual.reshape(1, blocks, 2, elec)
 
 

time: 51.3 us -> 52.4 us (1.021)
  Pallas kernels: 47.8 us -> 51 us
  local copies, waits for them, and re-layouts: 1.97 us -> 0 us
    pallas_call x0 -> x1, Pallas kernels: none -> 3.64 us  [body(): pl.pallas_call(gather_up, out_shape=(jax.ShapeDtypeStruct((nx, ny // n_in...]
    unnamed x4 -> x0, local copies, waits for them, and re-layouts: 1.97 us -> none
where the time goes in v5:
time: 52.4 us; the launch traced here: 51.6 us
  Pallas kernels  51 us (97%)
  between operations  0.64 us (1%)
    pallas_call x1, Pallas kernels, body(): pl.pallas_call(functools.partial(kernel, n_space, n_inj, nx, ny, nz, bloc...  47.4 us
    pallas_call x1, Pallas kernels, body(): pl.pallas_call(gather_up, out_shape=(jax.ShapeDtypeStruct((nx, ny // n_in...  3.64 us

profile of v5, /device:TPU:1, one launch (start us, length us, event | category | flops | bytes accessed | tf_op | source)
XLA Modules:
  0.0 51.6 jit_solution(6633472478011636828)
XLA Ops:
  0.6 47.4 %shard_map.95 = (f32[2,8,3,8,128]{4,3,2,1,0:T(8,128)}, f32[64,128]{1,0:T(8,128)}) custom-call(f32[6,64,128]{2,1,0:T(8,128)} %sig_in.1, f32[2,6,64,128]{3,2,1,0:T(8,128)} %pot_in.1, f32[2,6,64,128]{3,2,1,0:T(8,128)} %adj_in.1, s32[2,2]{1,0:T(2,128)} %inj_in.1, s32[1,32]{1,0:T(1,128)} %bitcast.6, s32[1,32]{1,0:T(1,128)} %live_in.1, s32[64,128]{1,0:T(8,128)} %bitcast.4, ...), custom_call_target="tpu_custom_call" | custom-call | tf_op jit(solution)/shard_map/pallas_call | solution.py:503
  48.0 3.6 %shard_map.96 = (f32[6,8,128]{2,1,0:T(8,128)}, f32[64,128]{1,0:T(8,128)}) custom-call(f32[2,8,3,8,128]{4,3,2,1,0:T(8,128)} %get-tuple-element.6.shares, f32[64,128]{1,0:T(8,128)} %get-tuple-element.7.res_in), custom_call_target="tpu_custom_call" | custom-call | tf_op jit(solution)/shard_map/pallas_call | solution.py:543

commit v6 on v4

--- a/solution.py
+++ b/solution.py
@@ -171,15 +171,10 @@
         def _():
             buf[lead + (pl.ds(H - width if low_side else nx + H, width), rows)] = nothing
 
-    chunk = ny // 2
+    chunk = ny
 
     def in_chunks(work):
-        def step(q, carry):
-            low = pl.multiple_of(q * chunk, 8)
-            work(low, pl.ds(pl.multiple_of(low + PAD, 8), chunk))
-            return carry
-
-        lax.fori_loop(0, ny // chunk, step, 0)
+        work(0, pl.ds(PAD, ny))
 
     first_lane = iota((chunk, nz), 1) == 0
     last_lane = iota((chunk, nz), 1) == nz - 1
@@ -489,8 +484,8 @@
     gradient, residual = pl.pallas_call(
         functools.partial(kernel, n_space, n_inj, nx, ny, nz, blocks),
         out_shape=(
-            jax.ShapeDtypeStruct((nx, ny // n_inj, nz), F32),
-            jax.ShapeDtypeStruct((2 * blocks, elec), F32),
+            pltpu.VMEM((nx, ny // n_inj, nz), F32),
+            pltpu.VMEM((2 * blocks, elec), F32),
         ),
         in_specs=[hbm] * 8,
         out_specs=(vmem, vmem),

time: 51.3 us -> 48.8 us (0.951)
  the two profiles are of different devices: /device:TPU:1 before, /device:TPU:8 now
where the time goes in v6:
time: 48.8 us
  Pallas kernels  46.9 us (96%)
  local copies, waits for them, and re-layouts  1.22 us (2%)
  between operations  0.64 us (1%)
    pallas_call x1, Pallas kernels, body(): pl.pallas_call(functools.partial(kernel, n_space, n_inj, nx, ny, nz, bloc...  46.9 us
    unnamed x2, local copies, waits for them, and re-layouts  1.22 us

profile of v6, /device:TPU:8, one launch (start us, length us, event | category | flops | bytes accessed | tf_op | source)
XLA Modules:
  0.0 48.8 jit_solution(7269300517096718212)
XLA Ops:
  0.6 46.9 %shard_map.95 = (f32[6,8,128]{2,1,0:T(8,128)S(1)}, f32[64,128]{1,0:T(8,128)S(1)}) custom-call(f32[6,64,128]{2,1,0:T(8,128)} %sig_in.1, f32[2,6,64,128]{3,2,1,0:T(8,128)} %pot_in.1, f32[2,6,64,128]{3,2,1,0:T(8,128)} %adj_in.1, s32[2,2]{1,0:T(2,128)} %inj_in.1, s32[1,32]{1,0:T(1,128)} %bitcast.7, s32[1,32]{1,0:T(1,128)} %live_in.1, s32[64,128]{1,0:T(8,128)} %bitcast.5, ...), custom_call_target="tpu_custom_call" | custom-call | tf_op jit(solution)/shard_map/pallas_call | solution.py:484
  47.5 0.6 %copy.12 = f32[6,8,128]{2,1,0:T(8,128)} copy(f32[6,8,128]{2,1,0:T(8,128)S(1)} %get-tuple-element.6) | data formatting | bytes 49152
  48.1 0.6 %copy.13 = f32[1,32,2,128]{3,2,1,0:T(2,128)} copy(f32[1,32,2,128]{3,2,1,0:T(2,128)S(1)} %bitcast.4) | data formatting | bytes 65536

commit v7 on v6

--- a/solution.py
+++ b/solution.py
@@ -88,35 +88,6 @@
         for buf in (pa, pb, aa, ab):
             buf[:, :, pl.ds(low, PAD), :] = jnp.zeros((2, planes, PAD, nz), F32)
 
-    pl.semaphore_wait(barrier, n_space - 1 + n_inj - 1)
-
-    def remote(source, target, send_sem, recv_sem, space, inj):
-        return pltpu.make_async_remote_copy(
-            src_ref=source, dst_ref=target, send_sem=send_sem, recv_sem=recv_sem,
-            device_id=(space, inj), device_id_type=MESH,
-        )
-
-    def pair(source, target, lead, width, send_sems, recv_sems, k):
-        return [
-            remote(
-                source.at[lead + (pl.ds(nx - width, width),)], target.at[lead + (pl.ds(H - width, width), rows)],
-                send_sems.at[k], recv_sems.at[k], right, my_inj,
-            ),
-            remote(
-                source.at[lead + (pl.ds(0, width),)], target.at[lead + (pl.ds(nx + H, width), rows)],
-                send_sems.at[k + 1], recv_sems.at[k + 1], left, my_inj,
-            ),
-        ]
-
-    early = pair(sig_in, sigma, (), 3, halo_send, halo_recv, 0)
-    near = [pair(pot_in, pa, (i,), 3, halo_send, halo_recv, 2 + 2 * i) for i in range(2)]
-    late = [
-        remote(sig_in.at[pl.ds(nx - H, 1)], sigma.at[pl.ds(0, 1), rows], far_send.at[0], far_recv.at[0], right, my_inj),
-        remote(sig_in.at[pl.ds(H - 1, 1)], sigma.at[pl.ds(planes - 1, 1), rows], far_send.at[1], far_recv.at[1], left, my_inj),
-    ] + pair(adj_in, aa, (slice(None),), H, far_send, far_recv, 2)
-    for copy in early + near[0]:
-        copy.start()
-
     for copy in small:
         copy.wait()
     lanes = 4 * blocks
@@ -145,14 +116,41 @@
     for t in range(n_space):
         send[t] = packed[8 * t : 8 * t + 8]
 
+    pl.semaphore_wait(barrier, n_space - 1 + n_inj - 1)
+
+    def remote(source, target, send_sem, recv_sem, space, inj):
+        return pltpu.make_async_remote_copy(
+            src_ref=source, dst_ref=target, send_sem=send_sem, recv_sem=recv_sem,
+            device_id=(space, inj), device_id_type=MESH,
+        )
+
+    def pair(source, target, lead, width, send_sems, recv_sems, k):
+        return [
+            remote(
+                source.at[lead + (pl.ds(nx - width, width),)], target.at[lead + (pl.ds(H - width, width), rows)],
+                send_sems.at[k], recv_sems.at[k], right, my_inj,
+            ),
+            remote(
+                source.at[lead + (pl.ds(0, width),)], target.at[lead + (pl.ds(nx + H, width), rows)],
+                send_sems.at[k + 1], recv_sems.at[k + 1], left, my_inj,
+            ),
+        ]
+
+    early = pair(sig_in, sigma, (), 3, halo_send, halo_recv, 0)
+    near = [pair(pot_in, pa, (i,), 3, halo_send, halo_recv, 2 + 2 * i) for i in range(2)]
+    late = [
+        remote(sig_in.at[pl.ds(nx - H, 1)], sigma.at[pl.ds(0, 1), rows], far_send.at[0], far_recv.at[0], right, my_inj),
+        remote(sig_in.at[pl.ds(H - 1, 1)], sigma.at[pl.ds(planes - 1, 1), rows], far_send.at[1], far_recv.at[1], left, my_inj),
+    ] + pair(adj_in, aa, (slice(None),), H, far_send, far_recv, 2)
+    for copy in early + near[0]:
+        copy.start()
+
     def send_block(d, carry):
         to = lax.rem(me + d, n_space)
         remote(send.at[to], recv.at[me], block_send, block_recv, to, my_inj).start()
         return carry
 
     lax.fori_loop(1, n_space, send_block, 0)
-    for copy in near[1]:
-        copy.start()
     recv[me] = send[me]
 
     cell_ids = iota((ny, nz), 0) * nz + iota((ny, nz), 1)
@@ -241,6 +239,9 @@
     def finish_potential(i):
         for copy in near[i]:
             copy.wait()
+        if i == 0:
+            for copy in near[1]:
+                copy.start()
         beyond(pa, (i,), True, 3)
         beyond(pa, (i,), False, 3)
         sweep(i, src, pa, pb, [2, 3, 4, end - 4, end - 3, end - 2], w0)

time: 48.8 us -> 48.1 us (0.986)
  the two profiles are of different devices: /device:TPU:8 before, /device:TPU:1 now
where the time goes in v7:
time: 48.1 us; the launch traced here: 47.6 us
  Pallas kernels  45.8 us (95%)
  local copies, waits for them, and re-layouts  1.22 us (3%)
  between operations  0.64 us (1%)
    pallas_call x1, Pallas kernels, body(): pl.pallas_call(functools.partial(kernel, n_space, n_inj, nx, ny, nz, bloc...  45.8 us
    unnamed x2, local copies, waits for them, and re-layouts  1.22 us

profile of v7, /device:TPU:1, one launch (start us, length us, event | category | flops | bytes accessed | tf_op | source)
XLA Modules:
  0.0 47.6 jit_solution(5261007793224362687)
XLA Ops:
  0.6 45.8 %shard_map.95 = (f32[6,8,128]{2,1,0:T(8,128)S(1)}, f32[64,128]{1,0:T(8,128)S(1)}) custom-call(f32[6,64,128]{2,1,0:T(8,128)} %sig_in.1, f32[2,6,64,128]{3,2,1,0:T(8,128)} %pot_in.1, f32[2,6,64,128]{3,2,1,0:T(8,128)} %adj_in.1, s32[2,2]{1,0:T(2,128)} %inj_in.1, s32[1,32]{1,0:T(1,128)} %bitcast.7, s32[1,32]{1,0:T(1,128)} %live_in.1, s32[64,128]{1,0:T(8,128)} %bitcast.5, ...), custom_call_target="tpu_custom_call" | custom-call | tf_op jit(solution)/shard_map/pallas_call | solution.py:485
  46.4 0.6 %copy.12 = f32[6,8,128]{2,1,0:T(8,128)} copy(f32[6,8,128]{2,1,0:T(8,128)S(1)} %get-tuple-element.6) | data formatting | bytes 49152
  47.0 0.6 %copy.13 = f32[1,32,2,128]{3,2,1,0:T(2,128)} copy(f32[1,32,2,128]{3,2,1,0:T(2,128)S(1)} %bitcast.4) | data formatting | bytes 65536

commit v8 on v7

--- a/solution.py
+++ b/solution.py
@@ -142,7 +142,7 @@
         remote(sig_in.at[pl.ds(nx - H, 1)], sigma.at[pl.ds(0, 1), rows], far_send.at[0], far_recv.at[0], right, my_inj),
         remote(sig_in.at[pl.ds(H - 1, 1)], sigma.at[pl.ds(planes - 1, 1), rows], far_send.at[1], far_recv.at[1], left, my_inj),
     ] + pair(adj_in, aa, (slice(None),), H, far_send, far_recv, 2)
-    for copy in early + near[0]:
+    for copy in early:
         copy.start()
 
     def send_block(d, carry):
@@ -151,6 +151,8 @@
         return carry
 
     lax.fori_loop(1, n_space, send_block, 0)
+    for copy in near[0]:
+        copy.start()
     recv[me] = send[me]
 
     cell_ids = iota((ny, nz), 0) * nz + iota((ny, nz), 1)

time: 48.1 us -> 49.4 us (1.027)
  Pallas kernels: 45.8 us -> 47.4 us
    pallas_call x1, Pallas kernels: 45.8 us -> 47.4 us  [body(): pl.pallas_call(functools.partial(kernel, n_space, n_inj, nx, ny, nz, bloc...]
where the time goes in v8:
time: 49.4 us; the launch traced here: 49.3 us
  Pallas kernels  47.4 us (96%)
  local copies, waits for them, and re-layouts  1.22 us (2%)
  between operations  0.64 us (1%)
    pallas_call x1, Pallas kernels, body(): pl.pallas_call(functools.partial(kernel, n_space, n_inj, nx, ny, nz, bloc...  47.4 us
    unnamed x2, local copies, waits for them, and re-layouts  1.22 us

profile of v8, /device:TPU:1, one launch (start us, length us, event | category | flops | bytes accessed | tf_op | source)
XLA Modules:
  0.0 49.3 jit_solution(11490468122577848400)
XLA Ops:
  0.6 47.4 %shard_map.95 = (f32[6,8,128]{2,1,0:T(8,128)S(1)}, f32[64,128]{1,0:T(8,128)S(1)}) custom-call(f32[6,64,128]{2,1,0:T(8,128)} %sig_in.1, f32[2,6,64,128]{3,2,1,0:T(8,128)} %pot_in.1, f32[2,6,64,128]{3,2,1,0:T(8,128)} %adj_in.1, s32[2,2]{1,0:T(2,128)} %inj_in.1, s32[1,32]{1,0:T(1,128)} %bitcast.7, s32[1,32]{1,0:T(1,128)} %live_in.1, s32[64,128]{1,0:T(8,128)} %bitcast.5, ...), custom_call_target="tpu_custom_call" | custom-call | tf_op jit(solution)/shard_map/pallas_call | solution.py:487
  48.1 0.6 %copy.12 = f32[6,8,128]{2,1,0:T(8,128)} copy(f32[6,8,128]{2,1,0:T(8,128)S(1)} %get-tuple-element.6) | data formatting | bytes 49152
  48.7 0.6 %copy.13 = f32[1,32,2,128]{3,2,1,0:T(2,128)} copy(f32[1,32,2,128]{3,2,1,0:T(2,128)S(1)} %bitcast.4) | data formatting | bytes 65536
